TPU v7x, 128 devices: a whole 4x4x4 slice. The times are simulated.
128 devices in a mesh: pool: 8 (over z, y_hi), seq: 16 (over x, y_lo, core).
Axes of the slice: x: 4, y: 4 (y_hi: 2, y_lo: 2; y = y_hi * 2 + y_lo), z: 4, core: 2. Of those that a mesh axis runs over, the one named last changes fastest.
Arguments:
- patches: bfloat16 [8192, 1280], P(('pool', 'seq')), may hold values from -6 to 6
- merge_up: bfloat16 [5120, 5120], P(None, 'seq'), may hold values from -0.078125 to 0.078125
- merge_down: bfloat16 [5120, 8192], P('seq'), may hold values from -0.078125 to 0.078125
- image_pos: int32 [2048], P(('pool', 'seq')), may hold values from 0 to 6143, as said below
- text_rows: bfloat16 [6144, 8192], P('seq'), may hold values from -6 to 6
- segment: int32 [6144], P('seq'), may hold values from 0 to 3, never falling along the last dimension, each value on 1 to 4608 neighbouring positions
- query_weight: bfloat16 [8192, 8192], P('seq', 'pool')
- key_weight: bfloat16 [8192, 1024], P('seq', 'pool')
- value_weight: bfloat16 [8192, 1024], P('seq', 'pool'), may hold values from -0.0625 to 0.0625
Outputs:
- attended: bfloat16 [6144, 8192], P('seq', 'pool')
Inputs may be any that keep to these rules, and one draw needn't show every extreme that they name: `image_pos`: positions are all distinct. Of the 16 image tokens of one device, at most 2 lie in one block of 384 positions, and in every device's tokens some block holds exactly 2. `segment`: request numbers never fall along the sequence.
All inputs are finite; a program needn't handle non-finite values.
Results may differ from a plain program's by a relative error of at most 0.02.
The roundings to bfloat16 on the way count: a program that leaves them out, or rounds other values in their place, can miss the bound.
Values may be sent and summed in bfloat16 or wider, within the bound.
No kernel may reach another device: no remote copies, remote signals or barrier semaphores. Data moves between devices by JAX's collectives and lax.ppermute only.
A program may use at most 128 MiB of HBM per device.

v0:
```python
import jax
import jax.numpy as jnp
from jax import lax
from jax.experimental import pallas as pl
from jax.experimental.pallas import tpu as pltpu
from jax.sharding import PartitionSpec as P

HD = 128
CAP = 2
AUX = 128
NORM_EPS = 1e-06
ROPE_BASE = 1000000.0
BIG_NEG = -1e30
LOG2E = 1.4426950408889634
VMEM_BYTES = 56 * 1024 * 1024
X, Y, C = 4, 2, 2
Z, YH = 4, 2
CHUNK = 1024


def rms_rows(matrix):
    return matrix * lax.rsqrt(jnp.mean(matrix * matrix, axis=-1, keepdims=True) + NORM_EPS)


def seq_shift(array, dx, dy, dc):
    pairs = []
    for source in range(X * Y * C):
        x, y, c = source // (Y * C), source // C % Y, source % C
        pairs.append((source, ((x + dx) % X) * Y * C + (y ^ dy) * C + (c ^ dc)))
    return lax.ppermute(array, "seq", pairs)


HALF_D = 4096


def pool_shift(array, dz, dy):
    pairs = []
    for source in range(Z * YH):
        z, y = source // YH, source % YH
        pairs.append((source, ((z + dz) % Z) * YH + (y ^ dy)))
    return lax.ppermute(array, "pool", pairs)


def whole(shape):
    return pl.BlockSpec(shape, lambda n: (0, 0), pipeline_mode=pl.Buffered(1))


def patch_kernel(patches_ref, segment_ref, out_ref):
    own = out_ref.shape[0]
    patch_count, width = patches_ref.shape
    normed = rms_rows(patches_ref[...].astype(jnp.float32)).astype(jnp.bfloat16)
    token = lax.broadcasted_iota(jnp.int32, (own, patch_count), 0)
    patch = lax.broadcasted_iota(jnp.int32, (own, patch_count), 1)
    for k in range(4):
        pick = jnp.where(patch == 4 * token + k, 1.0, 0.0).astype(jnp.bfloat16)
        out_ref[:, k * width:(k + 1) * width] = jnp.dot(
            pick, normed, preferred_element_type=jnp.float32
        ).astype(jnp.bfloat16)
    lane = lax.broadcasted_iota(jnp.int32, (own, AUX), 1)
    marks = jnp.zeros((own, AUX), jnp.float32)
    for v in range(1, 4):
        before = jnp.sum(jnp.where(segment_ref[...] < v, 1.0, 0.0), axis=1, keepdims=True)
        high = jnp.floor(before * (1.0 / 128.0))
        marks += jnp.where(lane == v - 1, high, 0.0) + jnp.where(lane == v + 2, before - 128.0 * high, 0.0)
    out_ref[:, 4 * width:] = marks.astype(jnp.bfloat16)


def prepare(patches, segment):
    vmem = pl.BlockSpec(memory_space=pltpu.VMEM)
    return pl.pallas_call(
        patch_kernel,
        in_specs=[vmem, vmem],
        out_specs=vmem,
        out_shape=jax.ShapeDtypeStruct((patches.shape[0] // 4, 4 * patches.shape[1] + AUX), jnp.bfloat16),
        name="prepare",
    )(patches, segment[None, :])


def merger_kernel(*refs):
    pieces, (up_a, up_b, down_a, down_b), outs = refs[:X], refs[X:X + 4], refs[X + 4:X + 4 + X + Y]
    hidden_ref = refs[-1]
    rows = pieces[0].shape[0]
    depth = up_a.shape[1]
    step = pl.program_id(0)
    half = pl.num_programs(0) // 2

    @pl.when(step == 0)
    def _():
        merged = jnp.concatenate([piece[:, :depth] for piece in pieces], axis=0)
        up = jnp.concatenate([up_a[...], up_b[...]], axis=0)
        value = lax.dot_general(merged, up, (((1,), (1,)), ((), ())), preferred_element_type=jnp.float32)
        value = 0.5 * value * (1.0 + lax.erf(value * (0.5 ** 0.5)))
        hidden_ref[...] = value.astype(jnp.bfloat16)

    down = jnp.concatenate([down_a[...], down_b[...]], axis=0)
    total = jnp.dot(hidden_ref[...], down, preferred_element_type=jnp.float32)

    @pl.when(step < half)
    def _():
        for dx in range(X):
            outs[dx][...] = total[dx * rows:(dx + 1) * rows].astype(outs[dx].dtype)

    @pl.when(step >= half)
    def _():
        own = rows // Y
        for dx in range(X):
            for dy in range(Y):
                at = dx * rows + dy * own
                outs[X + dy][dx * own:(dx + 1) * own, :] = total[at:at + own].astype(outs[X + dy].dtype)


def merger(pieces, ups, downs):
    rows = pieces[0].shape[0]
    units, depth = ups[0].shape
    width = downs[0].shape[1]
    block = 1024
    half = HALF_D // block
    first = lambda shape: pl.BlockSpec(shape, lambda n: (0, jnp.minimum(n, half - 1)))
    second = lambda shape: pl.BlockSpec(shape, lambda n: (0, jnp.maximum(n - half, 0)))
    own = rows // Y
    shape = jax.ShapeDtypeStruct
    return pl.pallas_call(
        merger_kernel,
        grid=(width // block,),
        in_specs=[whole(pieces[0].shape)] * X
        + [whole((units, depth))] * 2
        + [pl.BlockSpec((units, block), lambda n: (0, n))] * 2,
        out_specs=[first((rows, block))] * X + [second((X * own, block))] * Y,
        out_shape=[shape((rows, HALF_D), jnp.float32 if dx == 0 else jnp.bfloat16) for dx in range(X)]
        + [shape((X * own, width - HALF_D), jnp.float32 if dy == 0 else jnp.bfloat16) for dy in range(Y)],
        scratch_shapes=[pltpu.VMEM((X * rows, 2 * units), jnp.bfloat16)],
        compiler_params=pltpu.CompilerParams(vmem_limit_bytes=VMEM_BYTES),
        name="merger",
    )(*pieces, *ups, *downs)


def turned(part, cosine, sine):
    return part * cosine + pltpu.roll(part, HD // 2, 1) * sine


def slot_marks(b0, b1):
    cap = b0.shape[0] // Z
    at = b0.shape[1] - AUX
    blocks = []
    for dz in range(Z):
        for ref in (b0, b1):
            blocks.append(ref[dz * cap:(dz + 1) * cap, at:])
    return jnp.concatenate(blocks, axis=0), jnp.concatenate([b0[:, at:], b1[:, at:]], axis=0)


def slot_pick(marks, rows):
    value = marks.astype(jnp.float32)
    offset = value[:, 0:1] * 128.0 + value[:, 1:2]
    offset = jnp.where(value[:, 2:3] > 0.5, offset, -1.0).astype(jnp.int32)
    token = lax.broadcasted_iota(jnp.int32, (value.shape[0], rows), 1)
    return jnp.where(offset == token, 1.0, 0.0).T.astype(jnp.bfloat16)


def lane_sums(matrix):
    total = matrix[:, :HD]
    for at in range(HD, matrix.shape[1], HD):
        total += matrix[:, at:at + HD]
    return total


def text_kernel(text_ref, weight_ref, kv_ref, total_ref):
    @pl.when(pl.program_id(0) == 0)
    def _():
        kv_ref[...] = jnp.zeros_like(kv_ref)
        total_ref[...] = jnp.zeros_like(total_ref)

    kv_ref[...] += jnp.dot(text_ref[...], weight_ref[...], preferred_element_type=jnp.float32)
    value = text_ref[...].astype(jnp.float32)
    total_ref[...] += lane_sums(value * value)


def project_text(text_rows, weights):
    rows, width = text_rows.shape
    kv_block = weights.shape[1] // (2 * HD) - 1
    shape = jax.ShapeDtypeStruct
    return pl.pallas_call(
        text_kernel,
        grid=(width // CHUNK,),
        in_specs=[
            pl.BlockSpec((rows, CHUNK), lambda n: (0, n)),
            pl.BlockSpec((CHUNK, 2 * HD), lambda n: (n, kv_block)),
        ],
        out_specs=[whole((rows, 2 * HD)), whole((rows, HD))],
        out_shape=[shape((rows, 2 * HD), jnp.float32), shape((rows, HD), jnp.float32)],
        compiler_params=pltpu.CompilerParams(vmem_limit_bytes=VMEM_BYTES),
        name="project_text",
    )(text_rows, weights)


def slot_kernel(
    a0, a1, a2, a3, b0, b1, weight_ref, text_kv_ref, text_total_ref, cos_ref, sin_ref,
    kv_ref, scale_ref, sum_ref, total_ref,
):
    rows = text_kv_ref.shape[0]
    step = pl.program_id(0)
    steps = pl.num_programs(0)
    half = HALF_D // CHUNK
    width = steps * CHUNK

    @pl.when(step == 0)
    def _():
        sum_ref[...] = jnp.zeros_like(sum_ref)
        total_ref[...] = jnp.zeros_like(total_ref)

    def add(at, refs, index):
        part = pl.ds(pl.multiple_of(index * CHUNK, CHUNK), CHUNK)
        slots = jnp.concatenate([ref[:, part] for ref in refs], axis=0)
        sum_ref[at] += jnp.dot(slots, weight_ref[...], preferred_element_type=jnp.float32)
        value = slots.astype(jnp.float32)
        total_ref[at] += lane_sums(value * value)

    @pl.when(step < half)
    def _():
        add(0, (a0, a1, a2, a3), step)

    @pl.when(step >= half)
    def _():
        add(1, (b0, b1), step - half)

    @pl.when(step == steps - 1)
    def _():
        marks = slot_marks(b0, b1)[1]
        pick = slot_pick(marks, rows)
        held = jnp.dot(pick, marks, preferred_element_type=jnp.float32)[:, 2:3] > 0.5
        cap = marks.shape[0] // (Z * YH)

        def joined(ref):
            first = [
                ref[0, (dz * YH + yh) * cap:(dz * YH + yh + 1) * cap, :] for yh in range(YH) for dz in range(Z)
            ]
            return jnp.concatenate(first, axis=0) + ref[1]

        def placed(value):
            high = value.astype(jnp.bfloat16)
            low = (value - high.astype(jnp.float32)).astype(jnp.bfloat16)
            return jnp.dot(pick, high, preferred_element_type=jnp.float32) + jnp.dot(
                pick, low, preferred_element_type=jnp.float32
            )

        def scale_of(total):
            return lax.rsqrt(jnp.sum(total, axis=1, keepdims=True) / width + NORM_EPS)

        slot_scale = scale_of(joined(total_ref))
        text_scale = scale_of(text_total_ref[...])
        slot_scale = jnp.broadcast_to(slot_scale, (slot_scale.shape[0], HD))
        scale = jnp.where(held, placed(slot_scale), text_scale)
        scale_ref[...] = scale
        kv = jnp.where(held, placed(joined(sum_ref)), text_kv_ref[...])
        kv_ref[:, :HD] = turned(kv[:, :HD] * scale, cos_ref[...], sin_ref[...]).astype(jnp.bfloat16)
        kv_ref[:, HD:] = (kv[:, HD:] * scale).astype(jnp.bfloat16)


def project_slots(slots_a, slots_b, weights, text_kv, text_total, cosine, sine):
    rows = text_kv.shape[0]
    width = weights.shape[0]
    slot_count = X * slots_a[0].shape[0]
    kv_block = weights.shape[1] // (2 * HD) - 1
    shape = jax.ShapeDtypeStruct
    return pl.pallas_call(
        slot_kernel,
        grid=(width // CHUNK,),
        in_specs=[whole(piece.shape) for piece in slots_a]
        + [whole(piece.shape) for piece in slots_b]
        + [pl.BlockSpec((CHUNK, 2 * HD), lambda n: (n, kv_block))]
        + [whole((rows, 2 * HD)), whole((rows, HD)), whole((rows, HD)), whole((rows, HD))],
        out_specs=[whole((rows, 2 * HD)), whole((rows, HD))],
        out_shape=[shape((rows, 2 * HD), jnp.bfloat16), shape((rows, HD), jnp.float32)],
        scratch_shapes=[
            pltpu.VMEM((2, slot_count, 2 * HD), jnp.float32),
            pltpu.VMEM((2, slot_count, HD), jnp.float32),
        ],
        compiler_params=pltpu.CompilerParams(vmem_limit_bytes=VMEM_BYTES),
        name="project_slots",
    )(*slots_a, *slots_b, weights, text_kv, text_total, cosine, sine)


GROUP = 2
SOFT = HD ** (-0.5) * LOG2E
LIMIT = 60.0


def query_kernel(
    text_ref, a0, a1, a2, a3, b0, b1, weight_ref, scale_ref, cos_ref, sin_ref, kv_ref, start_ref,
    q_ref, top_ref, sum_ref, acc_ref, pick_a, pick_b, held_ref, total_ref,
):
    rows = text_ref.shape[0]
    step = pl.program_id(0)
    steps = pl.num_programs(0)
    half = HALF_D // CHUNK
    wide = GROUP * rows

    @pl.when(step == 0)
    def _():
        marks_a, marks_b = slot_marks(b0, b1)
        pick_a[...] = slot_pick(marks_a, rows)
        pick_b[...] = slot_pick(marks_b, rows)
        held_ref[...] = jnp.dot(pick_b[...], marks_b, preferred_element_type=jnp.float32)
        total_ref[...] = jnp.zeros_like(total_ref)

    def add(pick, refs, index):
        part = pl.ds(pl.multiple_of(index * CHUNK, CHUNK), CHUNK)
        slots = jnp.concatenate([ref[:, part] for ref in refs], axis=0)
        image = jnp.dot(pick[...], slots, preferred_element_type=jnp.float32)
        mixed = jnp.where(held_ref[:, 2:3] > 0.5, image, text_ref[...].astype(jnp.float32)).astype(jnp.bfloat16)
        total_ref[...] += jnp.dot(mixed, weight_ref[...], preferred_element_type=jnp.float32)

    @pl.when(step < half)
    def _():
        add(pick_a, (a0, a1, a2, a3), step)

    @pl.when(step >= half)
    def _():
        add(pick_b, (b0, b1), step - half)

    @pl.when(step == steps - 1)
    def _():
        heads = total_ref.shape[1] // HD
        for h in range(heads):
            part = total_ref[:, h * HD:(h + 1) * HD] * scale_ref[...]
            q_ref[h * rows:(h + 1) * rows, :] = turned(part, cos_ref[...], sin_ref[...]).astype(jnp.bfloat16)
        key_at = lax.broadcasted_iota(jnp.int32, (rows, rows), 0)
        query_at = lax.broadcasted_iota(jnp.int32, (rows, rows), 1)
        allowed = (key_at <= query_at) & (key_at >= start_ref[0:1, :])
        allowed = jnp.concatenate([allowed] * GROUP, axis=1)
        for g in range(heads // GROUP):
            part = slice(g * wide, (g + 1) * wide)
            scores = lax.dot_general(
                kv_ref[:, :HD], q_ref[part, :], (((1,), (1,)), ((), ())), preferred_element_type=jnp.float32
            )
            scores = jnp.where(allowed, scores, BIG_NEG)
            top = jnp.max(scores, axis=0, keepdims=True)
            probs = jnp.exp2((scores - top) * SOFT)
            top_ref[:, part] = top
            sum_ref[:, part] = jnp.sum(probs, axis=0, keepdims=True)
            acc_ref[:, part] = lax.dot_general(
                kv_ref[:, HD:], probs.astype(jnp.bfloat16), (((0,), (0,)), ((), ())),
                preferred_element_type=jnp.float32,
            )


def query(text_rows, slots_a, slots_b, weights, scale, cosine, sine, kv, starts, heads):
    rows, width = text_rows.shape
    slot_count = X * slots_a[0].shape[0]
    wide = heads * rows
    shape = jax.ShapeDtypeStruct
    return pl.pallas_call(
        query_kernel,
        grid=(width // CHUNK,),
        in_specs=[pl.BlockSpec((rows, CHUNK), lambda n: (0, n))]
        + [whole(piece.shape) for piece in slots_a]
        + [whole(piece.shape) for piece in slots_b]
        + [pl.BlockSpec((CHUNK, heads * HD), lambda n: (n, 0))]
        + [whole((rows, HD))] * 3
        + [whole((rows, 2 * HD)), whole((1, rows))],
        out_specs=[whole((wide, HD)), whole((1, wide)), whole((1, wide)), whole((HD, wide))],
        out_shape=[
            shape((wide, HD), jnp.bfloat16),
            shape((1, wide), jnp.float32),
            shape((1, wide), jnp.float32),
            shape((HD, wide), jnp.float32),
        ],
        scratch_shapes=[
            pltpu.VMEM((rows, slot_count), jnp.bfloat16),
            pltpu.VMEM((rows, slot_count), jnp.bfloat16),
            pltpu.VMEM((rows, AUX), jnp.float32),
            pltpu.VMEM((rows, heads * HD), jnp.float32),
        ],
        compiler_params=pltpu.CompilerParams(vmem_limit_bytes=VMEM_BYTES),
        name="query",
    )(text_rows, *slots_a, *slots_b, weights, scale, cosine, sine, kv, starts)


def attention_kernel(
    info_ref, q_ref, top_in, sum_in, acc_in, kv_ref, start_ref, out_ref, base_ref, top_ref, sum_ref, acc_ref
):
    rows = out_ref.shape[0]
    heads = out_ref.shape[1] // HD
    wide = GROUP * rows
    me = info_ref[0]
    first = info_ref[1]
    edge = info_ref[2]
    count = me - first

    def allowed_keys(indices):
        masks = []
        for index in indices:
            key_at = (index - me) * rows + lax.broadcasted_iota(jnp.int32, (rows, rows), 0)
            masks.append(key_at >= start_ref[0:1, :])
        return jnp.concatenate([jnp.concatenate(masks, axis=0)] * GROUP, axis=1)

    def loaded(indices):
        keys = jnp.concatenate([kv_ref[index, :, :HD] for index in indices], axis=0)
        values = jnp.concatenate([kv_ref[index, :, HD:] for index in indices], axis=0)
        return keys, values

    def scores_of(keys, part, allowed):
        scores = lax.dot_general(
            keys, q_ref[part, :], (((1,), (1,)), ((), ())), preferred_element_type=jnp.float32
        )
        return scores if allowed is None else jnp.where(allowed, scores, BIG_NEG)

    def mixed_of(values, probs):
        return lax.dot_general(
            values, probs.astype(jnp.bfloat16), (((0,), (0,)), ((), ())), preferred_element_type=jnp.float32
        )

    def fast(indices, masked):
        keys, values = loaded(indices)
        allowed = allowed_keys(indices) if masked else None
        for g in range(heads // GROUP):
            part = slice(g * wide, (g + 1) * wide)
            scores = scores_of(keys, part, allowed)
            top_ref[:, part] = jnp.maximum(top_ref[:, part], jnp.max(scores, axis=0, keepdims=True))
            probs = jnp.exp2(scores * SOFT - base_ref[:, part])
            acc_ref[:, part] += mixed_of(values, probs)
            sum_ref[:, part] += jnp.sum(probs, axis=0, keepdims=True)

    def slow(index):
        keys, values = loaded([index])
        allowed = allowed_keys([index])
        for g in range(heads // GROUP):
            part = slice(g * wide, (g + 1) * wide)
            scores = scores_of(keys, part, allowed)
            old = top_ref[:, part]
            top = jnp.maximum(old, jnp.max(scores, axis=0, keepdims=True))
            probs = jnp.exp2((scores - top) * SOFT)
            shrink = jnp.exp2((old - top) * SOFT)
            top_ref[:, part] = top
            sum_ref[:, part] = sum_ref[:, part] * shrink + jnp.sum(probs, axis=0, keepdims=True)
            acc_ref[:, part] = acc_ref[:, part] * shrink + mixed_of(values, probs)

    def start():
        top_ref[...] = top_in[...]
        sum_ref[...] = sum_in[...]
        acc_ref[...] = acc_in[...]

    def either(indices):
        needs = indices[-1] * rows < edge

        @pl.when(needs)
        def _():
            fast(indices, True)

        @pl.when(jnp.logical_not(needs))
        def _():
            fast(indices, False)

    start()
    base_ref[...] = top_in[...] * SOFT
    odd = count % 2

    @pl.when(odd == 1)
    def _():
        either([me - 1])

    def pair(i, _):
        at = me - 1 - odd - 2 * i
        either([at, at - 1])
        return 0

    lax.fori_loop(0, count // 2, pair, 0)
    grown = jnp.max(top_ref[...] * SOFT - base_ref[...])

    @pl.when(grown > LIMIT)
    def _():
        start()

        def again(i, _):
            slow(me - 1 - i)
            return 0

        lax.fori_loop(0, count, again, 0)

    for h in range(heads):
        part = slice(h * rows, (h + 1) * rows)
        out_ref[:, h * HD:(h + 1) * HD] = (acc_ref[:, part] / sum_ref[:, part]).T.astype(jnp.bfloat16)


def attend(info, state, kv_all, starts):
    rows = kv_all.shape[1]
    wide = state[0].shape[0]
    vmem = pl.BlockSpec(memory_space=pltpu.VMEM)
    return pl.pallas_call(
        attention_kernel,
        in_specs=[pl.BlockSpec(memory_space=pltpu.SMEM)] + [vmem] * 6,
        out_specs=vmem,
        out_shape=jax.ShapeDtypeStruct((rows, wide // rows * HD), jnp.bfloat16),
        scratch_shapes=[
            pltpu.VMEM((1, wide), jnp.float32),
            pltpu.VMEM((1, wide), jnp.float32),
            pltpu.VMEM((1, wide), jnp.float32),
            pltpu.VMEM((HD, wide), jnp.float32),
        ],
        compiler_params=pltpu.CompilerParams(vmem_limit_bytes=VMEM_BYTES),
        name="attend",
    )(info, *state, kv_all, starts)


def per_device(
    patches,
    merge_up,
    merge_down,
    image_pos,
    text_rows,
    segment,
    query_weight,
    key_weight,
    value_weight,
):
    seq_count = lax.axis_size("seq")
    seq_index = lax.axis_index("seq")
    rows, width = text_rows.shape
    bf16, f32 = jnp.bfloat16, jnp.float32

    with jax.named_scope("merger"):
        up_other = seq_shift(merge_up.T, 0, 0, 1)
        down_other = seq_shift(merge_down, 0, 0, 1)
        merged = prepare(patches, segment)
        own = merged.shape[0]
        beside = seq_shift(merged, 0, 1, 0)
        merged, query_weight, key_weight, value_weight = lax.optimization_barrier(
            (merged, query_weight, key_weight, value_weight)
        )
        weights = lax.all_gather(
            jnp.concatenate([query_weight, key_weight, value_weight], axis=1), "seq", axis=0, tiled=True
        )
        pair = jnp.concatenate([merged, beside], axis=0)
        pieces = [pair] + [seq_shift(pair, dx, 0, 0) for dx in range(1, X)]
        outs = merger(pieces, (merge_up.T, up_other), (merge_down, down_other))
        part_a, part_b = outs[:X], outs[X:]

    with jax.named_scope("sums"):
        got_a = [seq_shift(part_a[dx], -dx, 0, 0) for dx in range(1, X)]
        got_b = seq_shift(part_b[1], 0, 1, 0)
        sum_a = part_a[0] + sum(piece.astype(f32) for piece in got_a)
        sum_b = part_b[0] + got_b.astype(f32)
        last_a = seq_shift(sum_a[own:].astype(bf16), 0, 1, 0)
        last_b = [seq_shift(sum_b[dx * own:(dx + 1) * own].astype(bf16), -dx, 0, 0) for dx in range(1, X)]
        image_a = (sum_a[:own] + last_a.astype(f32)).astype(bf16)
        image_b = (sum_b[:own] + sum(piece.astype(f32) for piece in last_b)).astype(bf16)

    with jax.named_scope("segments"):
        counted = sum(
            piece[at:at + 1, merge_up.shape[0]:].astype(f32) for piece in pieces for at in range(0, Y * own, own)
        )
        counted = (counted + seq_shift(counted, 0, 0, 1))[0]
        ends = (counted[:3] * 128.0 + counted[3:6]).astype(jnp.int32)
        before = jnp.concatenate([jnp.zeros((1,), jnp.int32), ends])
        starts = jnp.sum(
            jnp.where(segment[None, :] == jnp.arange(4, dtype=jnp.int32)[:, None], before[:, None], 0), axis=0
        )
        info = jnp.stack([seq_index, starts[0] // rows, starts[-1]]).astype(jnp.int32)
        starts = (starts - seq_index * rows)[None, :]

    with jax.named_scope("angles"):
        positions = (seq_index * rows + jnp.arange(rows, dtype=jnp.int32)).astype(f32)
        frequency = ROPE_BASE ** (-(jnp.arange(HD // 2, dtype=f32) * 2.0 / HD))
        angles = positions[:, None] * frequency[None, :]
        cosine, sine = jnp.cos(angles), jnp.sin(angles)
        cosine = jnp.concatenate([cosine, cosine], axis=1)
        sine = jnp.concatenate([-sine, sine], axis=1)

    with jax.named_scope("route"):
        target = image_pos // rows
        offset = image_pos % rows
        matches = (target[:, None] == jnp.arange(seq_count, dtype=jnp.int32)[None, :]).astype(jnp.int32)
        slot_rank = jnp.sum((jnp.cumsum(matches, axis=0) - matches) * matches, axis=1)
        slot_index = target * CAP + slot_rank
        select = (slot_index[None, :] == jnp.arange(seq_count * CAP, dtype=jnp.int32)[:, None]).astype(bf16)
        marks = jnp.stack([offset // 128, offset % 128, jnp.ones_like(offset)], axis=1).astype(bf16)
        marks = jnp.pad(marks, ((0, 0), (0, AUX - 3)))
        send = jnp.dot(
            select, jnp.concatenate([image_a, image_b, marks], axis=1), preferred_element_type=f32
        ).astype(bf16)
        got = lax.all_to_all(
            send.reshape(seq_count, CAP, width + AUX), "seq", split_axis=0, concat_axis=0, tiled=True
        ).reshape(seq_count * CAP, width + AUX)
        got, info, starts, cosine, sine = lax.optimization_barrier((got, info, starts, cosine, sine))
        got_a, got_b = got[:, :HALF_D], got[:, HALF_D:]
        pair_a = jnp.concatenate([got_a, pool_shift(got_a, 0, 1)], axis=0)
        column_b = jnp.concatenate([got_b] + [pool_shift(got_b, dz, 0) for dz in range(1, Z)], axis=0)
        slots_a = [pair_a] + [pool_shift(pair_a, dz, 0) for dz in range(1, Z)]
        slots_b = [column_b, pool_shift(column_b, 0, 1)]

    with jax.named_scope("project"):
        text_kv, text_total = project_text(text_rows, weights)
        kv, scale = project_slots(slots_a, slots_b, weights, text_kv, text_total, cosine, sine)
        kv_all = lax.all_gather(kv, "seq", axis=0, tiled=True)
        state = query(
            text_rows, slots_a, slots_b, weights, scale, cosine, sine, kv, starts, query_weight.shape[1] // HD
        )

    with jax.named_scope("attend"):
        return attend(info, state, kv_all.reshape(seq_count, rows, 2 * HD), starts)


def solution(mesh):
    return jax.shard_map(
        per_device,
        mesh=mesh,
        in_specs=(
            P(("pool", "seq"), None),
            P(None, "seq"),
            P("seq", None),
            P(("pool", "seq")),
            P("seq", None),
            P("seq"),
            P("seq", "pool"),
            P("seq", "pool"),
            P("seq", "pool"),
        ),
        out_specs=P("seq", "pool"),
        check_vma=False,
    )
```

profile of v0, /device:TPU:6, one launch (start us, length us, event | category | flops | bytes accessed | tf_op | source)
XLA Modules:
  0.0 300.2 jit_solution(6358149355958593759)
XLA Ops:
  8.0 1.9 prepare.1
  9.9 2.6 pad_maximum_fusion
  15.5 3.8 %collective-permute-done = bf16[16,5248]{1,0:T(8,128)(2,1)} collective-permute-done((bf16[16,5248]{1,0:T(8,128)(2,1)S(1)}, bf16[16,5248]{1,0:T(8,128)(2,1)}, u32[]{:S(2)}, u32[]{:S(2)}) %collective-permute-start) | collective-permute-done | bytes 167968 | tf_op jit(solution)/shard_map/merger/ppermute | solution.py:30
  21.3 2.5 collective-permute-start.2
  24.6 14.0 %collective-permute-done.1.refs_1_ = bf16[32,5248]{1,0:T(8,128)(2,1)S(1)} collective-permute-done((bf16[32,5248]{1,0:T(8,128)(2,1)}, bf16[32,5248]{1,0:T(8,128)(2,1)S(1)}, u32[]{:S(2)}, u32[]{:S(2)}) %collective-permute-start.1) | collective-permute-done | bytes 335904 | tf_op jit(solution)/shard_map/merger/ppermute | solution.py:30
  38.6 1.8 collective-permute-done.2.refs_2_
  40.4 12.5 %collective-permute-done.3.refs_3_ = bf16[32,5248]{1,0:T(8,128)(2,1)S(1)} collective-permute-done((bf16[32,5248]{1,0:T(8,128)(2,1)}, bf16[32,5248]{1,0:T(8,128)(2,1)S(1)}, u32[]{:S(2)}, u32[]{:S(2)}) %collective-permute-start.3) | collective-permute-done | bytes 335904 | tf_op jit(solution)/shard_map/merger/ppermute | solution.py:30
  54.8 13.7 %merger.1 = (f32[32,4096]{1,0:T(8,128)}, bf16[32,4096]{1,0:T(8,128)(2,1)}, bf16[32,4096]{1,0:T(8,128)(2,1)}, bf16[32,4096]{1,0:T(8,128)(2,1)}, f32[64,4096]{1,0:T(8,128)}, /*index=5*/bf16[64,4096]{1,0:T(8,128)(2,1)}) custom-call(bf16[32,5248]{1,0:T(8,128)(2,1)} %constant_dynamic-update-slice_fusion.refs_0_, bf16[32,5248]{1,0:T(8,128)(2,1)} %copy-done.7, ...), custom_call_target="tpu_custom_call" | custom-call | tf_op jit(solution)/shard_map/merger/merger/pallas_call | solution.py:122
  70.2 2.8 collective-permute-start.7
  74.9 9.0 %collective-permute-done.8 = bf16[32,4096]{1,0:T(8,128)(2,1)S(1)} collective-permute-done((bf16[32,4096]{1,0:T(8,128)(2,1)}, bf16[32,4096]{1,0:T(8,128)(2,1)S(1)}, u32[]{:S(2)}, u32[]{:S(2)}) %collective-permute-start.8) | collective-permute-done | bytes 262176 | tf_op jit(solution)/shard_map/sums/ppermute | solution.py:30
  83.9 2.8 collective-permute-done.7
  86.7 10.0 %collective-permute-done.6 = bf16[32,4096]{1,0:T(8,128)(2,1)S(1)} collective-permute-done((bf16[32,4096]{1,0:T(8,128)(2,1)}, bf16[32,4096]{1,0:T(8,128)(2,1)S(1)}, u32[]{:S(2)}, u32[]{:S(2)}) %collective-permute-start.6) | collective-permute-done | bytes 262176 | tf_op jit(solution)/shard_map/sums/ppermute | solution.py:30
  99.7 1.9 collective-permute-start.13
  101.6 2.6 collective-permute-start.12
  104.2 2.2 collective-permute-done.9
  106.5 2.8 collective-permute-done.13
  109.3 3.0 %collective-permute-done.12 = bf16[16,4096]{1,0:T(8,128)(2,1)S(1)} collective-permute-done((bf16[16,4096]{1,0:T(8,128)(2,1)S(1)}, bf16[16,4096]{1,0:T(8,128)(2,1)S(1)}, u32[]{:S(2)}, u32[]{:S(2)}) %collective-permute-start.12) | collective-permute-done | bytes 131104 | tf_op jit(solution)/shard_map/sums/ppermute | solution.py:30
  112.3 3.6 %collective-permute-done.11 = bf16[16,4096]{1,0:T(8,128)(2,1)S(1)} collective-permute-done((bf16[16,4096]{1,0:T(8,128)(2,1)S(1)}, bf16[16,4096]{1,0:T(8,128)(2,1)S(1)}, u32[]{:S(2)}, u32[]{:S(2)}) %collective-permute-start.11) | collective-permute-done | bytes 131104 | tf_op jit(solution)/shard_map/sums/ppermute | solution.py:30
  117.2 6.4 %all-to-all-start = ((bf16[16,2,8320]{2,1,0:T(2,128)(2,1)}), bf16[16,2,8320]{2,1,0:T(2,128)(2,1)S(1)}, u32[]{:S(2)}, u32[]{:S(2)}) async-start(bf16[16,2,8320]{2,1,0:T(2,128)(2,1)} %reshape.49), calls=%async_computation | async-start | bytes 1064960 | tf_op jit(solution)/shard_map/route/all_to_all | solution.py:580
  128.3 10.0 %all-to-all-done = bf16[16,2,8320]{2,1,0:T(2,128)(2,1)S(1)} async-done(((bf16[16,2,8320]{2,1,0:T(2,128)(2,1)}), bf16[16,2,8320]{2,1,0:T(2,128)(2,1)S(1)}, u32[]{:S(2)}, u32[]{:S(2)}) %all-to-all-start) | async-done | bytes 532512 | tf_op jit(solution)/shard_map/route/all_to_all | solution.py:580
  138.6 4.4 %collective-permute-start.21 = (bf16[32,4224]{1,0:T(8,128)(2,1)S(1)}, bf16[32,4224]{1,0:T(8,128)(2,1)S(1)}, u32[]{:S(2)}, u32[]{:S(2)}) collective-permute-start(bf16[32,4224]{1,0:T(8,128)(2,1)S(1)} %slice.85), channel_id=1, source_target_pairs={{0,96},{16,112},{32,0},{48,16},{64,32},{80,48},{96,64},{112,80},{1... | collective-permute-start | bytes 811016 | tf_op jit(solution)/shard_map/route/ppermute | solution.py:41
  144.3 3.3 %collective-permute-start.15 = (bf16[32,4096]{1,0:T(8,128)(2,1)S(1)}, bf16[32,4096]{1,0:T(8,128)(2,1)S(1)}, u32[]{:S(2)}, u32[]{:S(2)}) collective-permute-start(bf16[32,4096]{1,0:T(8,128)(2,1)S(1)} %slice.84), channel_id=1, source_target_pairs={{0,16},{16,0},{32,48},{48,32},{64,80},{80,64},{96,112},{112,96},{1... | collective-permute-start | bytes 786440 | tf_op jit(solution)/shard_map/route/ppermute | solution.py:41
  147.5 6.7 %collective-permute-done.21 = bf16[32,4224]{1,0:T(8,128)(2,1)S(1)} collective-permute-done((bf16[32,4224]{1,0:T(8,128)(2,1)S(1)}, bf16[32,4224]{1,0:T(8,128)(2,1)S(1)}, u32[]{:S(2)}, u32[]{:S(2)}) %collective-permute-start.21) | collective-permute-done | bytes 270368 | tf_op jit(solution)/shard_map/route/ppermute | solution.py:41
  154.2 3.4 %collective-permute-done.19 = bf16[32,4224]{1,0:T(8,128)(2,1)S(1)} collective-permute-done((bf16[32,4224]{1,0:T(8,128)(2,1)S(1)}, bf16[32,4224]{1,0:T(8,128)(2,1)S(1)}, u32[]{:S(2)}, u32[]{:S(2)}) %collective-permute-start.19) | collective-permute-done | bytes 270368 | tf_op jit(solution)/shard_map/route/ppermute | solution.py:41
  157.7 3.2 %collective-permute-start.22 = (bf16[128,4224]{1,0:T(8,128)(2,1)S(1)}, bf16[128,4224]{1,0:T(8,128)(2,1)S(1)}, u32[]{:S(2)}, u32[]{:S(2)}) collective-permute-start(bf16[128,4224]{1,0:T(8,128)(2,1)S(1)} %pad_maximum_fusion.1.b0), channel_id=1, source_target_pairs={{0,16},{16,0},{32,48},{48,32},{64,80},{80,64},{96,112},{112,96},{1... | collective-permute-start | bytes 3244040 | tf_op jit(solution)/shard_map/route/ppermute | solution.py:41
  161.1 2.4 collective-permute-start.17
  164.8 9.4 %project_text.1 = (f32[384,256]{1,0:T(8,128)}, f32[384,128]{1,0:T(8,128)}) custom-call(bf16[384,8192]{1,0:T(8,128)(2,1)} %text_ref.3, bf16[8192,1280]{1,0:T(8,128)(2,1)} %all-gather.3.cloned.1.call-done.weight_ref), custom_call_target="tpu_custom_call" | custom-call | tf_op jit(solution)/shard_map/project/project_text/pallas_call | solution.py:181
  174.3 12.5 %collective-permute-done.16.a1 = bf16[64,4096]{1,0:T(8,128)(2,1)S(1)} collective-permute-done((bf16[64,4096]{1,0:T(8,128)(2,1)S(1)}, bf16[64,4096]{1,0:T(8,128)(2,1)S(1)}, u32[]{:S(2)}, u32[]{:S(2)}) %collective-permute-start.16) | collective-permute-done | bytes 524320 | tf_op jit(solution)/shard_map/route/ppermute | solution.py:41
  188.5 9.1 %project_slots.1 = (bf16[384,256]{1,0:T(8,128)(2,1)}, f32[384,128]{1,0:T(8,128)}) custom-call(bf16[64,4096]{1,0:T(8,128)(2,1)} %copy-done.1, bf16[64,4096]{1,0:T(8,128)(2,1)} %copy-done.4, bf16[64,4096]{1,0:T(8,128)(2,1)} %collective-permute-done.17.a2, bf16[64,4096]{1,0:T(8,128)(2,1)} %collective-permute-done.18.a3, bf16[128,4224]{1,0:T(8,128)(2,1)} %copy-done, ...), custom_call_target="tpu_custom_call" | custom-call | tf_op jit(solution)/shard_map/project/project_slots/pallas_call | solution.py:264
  197.7 19.7 %query.1 = (bf16[3072,128]{1,0:T(8,128)(2,1)}, f32[1,3072]{1,0:T(1,128)}, f32[1,3072]{1,0:T(1,128)}, f32[128,3072]{1,0:T(8,128)}) custom-call(bf16[384,8192]{1,0:T(8,128)(2,1)} %text_ref.3, bf16[64,4096]{1,0:T(8,128)(2,1)} %copy-done.1, bf16[64,4096]{1,0:T(8,128)(2,1)} %copy-done.4, bf16[64,4096]{1,0:T(8,128)(2,1)} %collective-permute-done.17.a2, ...), custom_call_target="tpu_custom_call" | custom-call | tf_op jit(solution)/shard_map/project/query/pallas_call | solution.py:351
  217.4 14.0 %all-gather.5.cloned.1.call-done = bf16[6144,256]{1,0:T(8,128)(2,1)} async-done(((bf16[384,256]{1,0:T(8,128)(2,1)}), bf16[6144,256]{1,0:T(8,128)(2,1)}) %all-gather.5.cloned.1.call-update) | async-done | bytes 3145744 | tf_op jit(solution)/shard_map/project/all_gather | solution.py:593
  231.3 62.0 %attend.1 = bf16[384,1024]{1,0:T(8,128)(2,1)} custom-call(s32[3]{0:T(128)} %pad_add_fusion.1.info_ref, bf16[3072,128]{1,0:T(8,128)(2,1)} %get-tuple-element.47.q_ref, f32[1,3072]{1,0:T(1,128)} %get-tuple-element.48.top_in, f32[1,3072]{1,0:T(1,128)} %get-tuple-element.49.sum_in, f32[128,3072]{1,0:T(8,128)} %get-tuple-element.50.acc_in, ...), custom_call_target="tpu_custom_call" | custom-call | tf_op jit(solution)/shard_map/attend/attend/pallas_call | solution.py:488
  (91 shorter events, 24.7 us)
Async XLA Ops:
  6.5 158.3 %all-gather.3.cloned.1.call-start = ((), (), s32[]{:S(2)}) async-start(), calls=%async_computation.1 | async-start | bytes 22282240 | tf_op jit(solution)/shard_map/merger/all_gather | solution.py:529
  12.4 42.4 %collective-permute-start.5 = (bf16[320,8192]{1,0:T(8,128)(2,1)}, bf16[320,8192]{1,0:T(8,128)(2,1)}, u32[]{:S(2)}, u32[]{:S(2)}) collective-permute-start(bf16[320,8192]{1,0:T(8,128)(2,1)} %refs_6_.1), channel_id=1, source_target_pairs={{0,1},{1,0},{2,3},{3,2},{4,5},{5,4},{6,7},{7,6},{8,9},{9,8},{10,11... | collective-permute-start | bytes 15728648 | tf_op jit(solution)/shard_map/merger/ppermute | solution.py:30
  12.5 6.8 %collective-permute-start = (bf16[16,5248]{1,0:T(8,128)(2,1)S(1)}, bf16[16,5248]{1,0:T(8,128)(2,1)}, u32[]{:S(2)}, u32[]{:S(2)}) collective-permute-start(bf16[16,5248]{1,0:T(8,128)(2,1)S(1)} %copy-done.6), channel_id=1, source_target_pairs={{0,2},{1,3},{2,0},{3,1},{4,6},{5,7},{6,4},{7,5},{8,10},{9,11},{10,... | collective-permute-start | bytes 503816 | tf_op jit(solution)/shard_map/merger/ppermute | solution.py:30
  14.2 40.6 %collective-permute-start.4 = (bf16[320,5120]{1,0:T(8,128)(2,1)S(1)}, bf16[320,5120]{1,0:T(8,128)(2,1)}, u32[]{:S(2)}, u32[]{:S(2)}) collective-permute-start(bf16[320,5120]{1,0:T(8,128)(2,1)S(1)} %bitcast.14), channel_id=1, source_target_pairs={{0,1},{1,0},{2,3},{3,2},{4,5},{5,4},{6,7},{7,6},{8,9},{9,8},{10,11... | collective-permute-start | bytes 9830408 | tf_op jit(solution)/shard_map/merger/ppermute | solution.py:30
  21.0 17.6 %collective-permute-start.1 = (bf16[32,5248]{1,0:T(8,128)(2,1)}, bf16[32,5248]{1,0:T(8,128)(2,1)S(1)}, u32[]{:S(2)}, u32[]{:S(2)}) collective-permute-start(bf16[32,5248]{1,0:T(8,128)(2,1)} %constant_dynamic-update-slice_fusion.refs_0_), channel_id=1, source_target_pairs={{0,4},{1,5},{2,6},{3,7},{4,8},{5,9},{6,10},{7,11},{8,12},{9,13},{1... | collective-permute-start | bytes 1007624 | tf_op jit(solution)/shard_map/merger/ppermute | solution.py:30
  21.3 19.1 %collective-permute-start.2 = (bf16[32,5248]{1,0:T(8,128)(2,1)}, bf16[32,5248]{1,0:T(8,128)(2,1)S(1)}, u32[]{:S(2)}, u32[]{:S(2)}) collective-permute-start(bf16[32,5248]{1,0:T(8,128)(2,1)} %constant_dynamic-update-slice_fusion.refs_0_), channel_id=1, source_target_pairs={{0,8},{1,9},{2,10},{3,11},{4,12},{5,13},{6,14},{7,15},{8,0},{9,1},... | collective-permute-start | bytes 1007624 | tf_op jit(solution)/shard_map/merger/ppermute | solution.py:30
  23.9 29.1 %collective-permute-start.3 = (bf16[32,5248]{1,0:T(8,128)(2,1)}, bf16[32,5248]{1,0:T(8,128)(2,1)S(1)}, u32[]{:S(2)}, u32[]{:S(2)}) collective-permute-start(bf16[32,5248]{1,0:T(8,128)(2,1)} %constant_dynamic-update-slice_fusion.refs_0_), channel_id=1, source_target_pairs={{0,12},{1,13},{2,14},{3,15},{4,0},{5,1},{6,2},{7,3},{8,4},{9,5},{1... | collective-permute-start | bytes 1007624 | tf_op jit(solution)/shard_map/merger/ppermute | solution.py:30
  38.6 15.0 %copy-start.7 = (bf16[32,5248]{1,0:T(8,128)(2,1)}, bf16[32,5248]{1,0:T(8,128)(2,1)S(1)}, u32[]{:S(2)}) copy-start(bf16[32,5248]{1,0:T(8,128)(2,1)S(1)} %collective-permute-done.1.refs_1_) | copy-start | bytes 1007620
  40.4 13.3 %copy-start.8 = (bf16[32,5248]{1,0:T(8,128)(2,1)}, bf16[32,5248]{1,0:T(8,128)(2,1)S(1)}, u32[]{:S(2)}) copy-start(bf16[32,5248]{1,0:T(8,128)(2,1)S(1)} %collective-permute-done.2.refs_2_) | copy-start | bytes 1007620
  53.6 1.2 collective-permute-start.14
  68.5 31.0 %copy-start.5 = (f32[64,4096]{1,0:T(8,128)S(1)}, f32[64,4096]{1,0:T(8,128)}, u32[]{:S(2)}) copy-start(f32[64,4096]{1,0:T(8,128)} %get-tuple-element.33) | copy-start | bytes 3145732
  68.5 15.4 %collective-permute-start.8 = (bf16[32,4096]{1,0:T(8,128)(2,1)}, bf16[32,4096]{1,0:T(8,128)(2,1)S(1)}, u32[]{:S(2)}, u32[]{:S(2)}) collective-permute-start(bf16[32,4096]{1,0:T(8,128)(2,1)} %get-tuple-element.32), channel_id=1, source_target_pairs={{0,4},{1,5},{2,6},{3,7},{4,8},{5,9},{6,10},{7,11},{8,12},{9,13},{1... | collective-permute-start | bytes 786440 | tf_op jit(solution)/shard_map/sums/ppermute | solution.py:30
  70.2 16.5 %collective-permute-start.7 = (bf16[32,4096]{1,0:T(8,128)(2,1)}, bf16[32,4096]{1,0:T(8,128)(2,1)S(1)}, u32[]{:S(2)}, u32[]{:S(2)}) collective-permute-start(bf16[32,4096]{1,0:T(8,128)(2,1)} %get-tuple-element.31), channel_id=1, source_target_pairs={{0,8},{1,9},{2,10},{3,11},{4,12},{5,13},{6,14},{7,15},{8,0},{9,1},... | collective-permute-start | bytes 786440 | tf_op jit(solution)/shard_map/sums/ppermute | solution.py:30
  73.0 23.6 %collective-permute-start.6 = (bf16[32,4096]{1,0:T(8,128)(2,1)}, bf16[32,4096]{1,0:T(8,128)(2,1)S(1)}, u32[]{:S(2)}, u32[]{:S(2)}) collective-permute-start(bf16[32,4096]{1,0:T(8,128)(2,1)} %get-tuple-element.30), channel_id=1, source_target_pairs={{0,12},{1,13},{2,14},{3,15},{4,0},{5,1},{6,2},{7,3},{8,4},{9,5},{1... | collective-permute-start | bytes 786440 | tf_op jit(solution)/shard_map/sums/ppermute | solution.py:30
  73.2 26.4 %collective-permute-start.10 = (bf16[64,4096]{1,0:T(8,128)(2,1)}, bf16[64,4096]{1,0:T(8,128)(2,1)S(1)}, u32[]{:S(2)}, u32[]{:S(2)}) collective-permute-start(bf16[64,4096]{1,0:T(8,128)(2,1)} %get-tuple-element.34), channel_id=1, source_target_pairs={{0,2},{1,3},{2,0},{3,1},{4,6},{5,7},{6,4},{7,5},{8,10},{9,11},{10,... | collective-permute-start | bytes 1572872 | tf_op jit(solution)/shard_map/sums/ppermute | solution.py:30
  97.8 8.7 %collective-permute-start.9 = (bf16[16,4096]{1,0:T(8,128)(2,1)S(1)}, bf16[16,4096]{1,0:T(8,128)(2,1)S(1)}, u32[]{:S(2)}, u32[]{:S(2)}) collective-permute-start(bf16[16,4096]{1,0:T(8,128)(2,1)S(1)} %slice.142), channel_id=1, source_target_pairs={{0,2},{1,3},{2,0},{3,1},{4,6},{5,7},{6,4},{7,5},{8,10},{9,11},{10,... | collective-permute-start | bytes 393224 | tf_op jit(solution)/shard_map/sums/ppermute | solution.py:30
  99.7 9.6 %collective-permute-start.13 = (bf16[16,4096]{1,0:T(8,128)(2,1)S(1)}, bf16[16,4096]{1,0:T(8,128)(2,1)S(1)}, u32[]{:S(2)}, u32[]{:S(2)}) collective-permute-start(bf16[16,4096]{1,0:T(8,128)(2,1)S(1)} %get-tuple-element.56), channel_id=1, source_target_pairs={{0,4},{1,5},{2,6},{3,7},{4,8},{5,9},{6,10},{7,11},{8,12},{9,13},{1... | collective-permute-start | bytes 393224 | tf_op jit(solution)/shard_map/sums/ppermute | solution.py:30
  101.6 10.6 %collective-permute-start.12 = (bf16[16,4096]{1,0:T(8,128)(2,1)S(1)}, bf16[16,4096]{1,0:T(8,128)(2,1)S(1)}, u32[]{:S(2)}, u32[]{:S(2)}) collective-permute-start(bf16[16,4096]{1,0:T(8,128)(2,1)S(1)} %get-tuple-element.57), channel_id=1, source_target_pairs={{0,8},{1,9},{2,10},{3,11},{4,12},{5,13},{6,14},{7,15},{8,0},{9,1},... | collective-permute-start | bytes 393224 | tf_op jit(solution)/shard_map/sums/ppermute | solution.py:30
  104.2 19.4 %copy-start.10 = (s32[384]{0:T(512)S(1)}, s32[384]{0:T(512)}, u32[]{:S(2)}) copy-start(s32[384]{0:T(512)} %param.14) | copy-start | bytes 4612
  104.2 11.6 %collective-permute-start.11 = (bf16[16,4096]{1,0:T(8,128)(2,1)S(1)}, bf16[16,4096]{1,0:T(8,128)(2,1)S(1)}, u32[]{:S(2)}, u32[]{:S(2)}) collective-permute-start(bf16[16,4096]{1,0:T(8,128)(2,1)S(1)} %get-tuple-element.55), channel_id=1, source_target_pairs={{0,12},{1,13},{2,14},{3,15},{4,0},{5,1},{6,2},{7,3},{8,4},{9,5},{1... | collective-permute-start | bytes 393224 | tf_op jit(solution)/shard_map/sums/ppermute | solution.py:30
  117.2 21.1 %all-to-all-start = ((bf16[16,2,8320]{2,1,0:T(2,128)(2,1)}), bf16[16,2,8320]{2,1,0:T(2,128)(2,1)S(1)}, u32[]{:S(2)}, u32[]{:S(2)}) async-start(bf16[16,2,8320]{2,1,0:T(2,128)(2,1)} %reshape.49), calls=%async_computation | async-start | bytes 1064960 | tf_op jit(solution)/shard_map/route/all_to_all | solution.py:580
  123.6 107.7 %all-gather.5.cloned.1.call-start = ((), (), s32[]{:S(2)}) async-start(), calls=%async_computation.2 | async-start | bytes 3342336 | tf_op jit(solution)/shard_map/project/all_gather | solution.py:593
  138.6 15.7 %collective-permute-start.21 = (bf16[32,4224]{1,0:T(8,128)(2,1)S(1)}, bf16[32,4224]{1,0:T(8,128)(2,1)S(1)}, u32[]{:S(2)}, u32[]{:S(2)}) collective-permute-start(bf16[32,4224]{1,0:T(8,128)(2,1)S(1)} %slice.85), channel_id=1, source_target_pairs={{0,96},{16,112},{32,0},{48,16},{64,32},{80,48},{96,64},{112,80},{1... | collective-permute-start | bytes 811016 | tf_op jit(solution)/shard_map/route/ppermute | solution.py:41
  142.9 11.3 %collective-permute-start.20 = (bf16[32,4224]{1,0:T(8,128)(2,1)S(1)}, bf16[32,4224]{1,0:T(8,128)(2,1)S(1)}, u32[]{:S(2)}, u32[]{:S(2)}) collective-permute-start(bf16[32,4224]{1,0:T(8,128)(2,1)S(1)} %slice.85), channel_id=1, source_target_pairs={{0,64},{16,80},{32,96},{48,112},{64,0},{80,16},{96,32},{112,48},{1... | collective-permute-start | bytes 811016 | tf_op jit(solution)/shard_map/route/ppermute | solution.py:41
  142.9 14.7 %collective-permute-start.19 = (bf16[32,4224]{1,0:T(8,128)(2,1)S(1)}, bf16[32,4224]{1,0:T(8,128)(2,1)S(1)}, u32[]{:S(2)}, u32[]{:S(2)}) collective-permute-start(bf16[32,4224]{1,0:T(8,128)(2,1)S(1)} %slice.85), channel_id=1, source_target_pairs={{0,32},{16,48},{32,64},{48,80},{64,96},{80,112},{96,0},{112,16},{1... | collective-permute-start | bytes 811016 | tf_op jit(solution)/shard_map/route/ppermute | solution.py:41
  144.3 16.7 %collective-permute-start.15 = (bf16[32,4096]{1,0:T(8,128)(2,1)S(1)}, bf16[32,4096]{1,0:T(8,128)(2,1)S(1)}, u32[]{:S(2)}, u32[]{:S(2)}) collective-permute-start(bf16[32,4096]{1,0:T(8,128)(2,1)S(1)} %slice.84), channel_id=1, source_target_pairs={{0,16},{16,0},{32,48},{48,32},{64,80},{80,64},{96,112},{112,96},{1... | collective-permute-start | bytes 786440 | tf_op jit(solution)/shard_map/route/ppermute | solution.py:41
  157.7 16.6 %copy-start = (bf16[128,4224]{1,0:T(8,128)(2,1)}, bf16[128,4224]{1,0:T(8,128)(2,1)S(1)}, u32[]{:S(2)}) copy-start(bf16[128,4224]{1,0:T(8,128)(2,1)S(1)} %pad_maximum_fusion.1.b0) | copy-start | bytes 3244036
  157.7 29.8 %collective-permute-start.22 = (bf16[128,4224]{1,0:T(8,128)(2,1)S(1)}, bf16[128,4224]{1,0:T(8,128)(2,1)S(1)}, u32[]{:S(2)}, u32[]{:S(2)}) collective-permute-start(bf16[128,4224]{1,0:T(8,128)(2,1)S(1)} %pad_maximum_fusion.1.b0), channel_id=1, source_target_pairs={{0,16},{16,0},{32,48},{48,32},{64,80},{80,64},{96,112},{112,96},{1... | collective-permute-start | bytes 3244040 | tf_op jit(solution)/shard_map/route/ppermute | solution.py:41
  161.0 13.3 %copy-start.1 = (bf16[64,4096]{1,0:T(8,128)(2,1)}, bf16[64,4096]{1,0:T(8,128)(2,1)S(1)}, u32[]{:S(2)}) copy-start(bf16[64,4096]{1,0:T(8,128)(2,1)S(1)} %pad_maximum_fusion.2.a0) | copy-start | bytes 1572868
  161.0 25.8 %collective-permute-start.16 = (bf16[64,4096]{1,0:T(8,128)(2,1)S(1)}, bf16[64,4096]{1,0:T(8,128)(2,1)S(1)}, u32[]{:S(2)}, u32[]{:S(2)}) collective-permute-start(bf16[64,4096]{1,0:T(8,128)(2,1)S(1)} %pad_maximum_fusion.2.a0), channel_id=1, source_target_pairs={{0,32},{16,48},{32,64},{48,80},{64,96},{80,112},{96,0},{112,16},{1... | collective-permute-start | bytes 1572872 | tf_op jit(solution)/shard_map/route/ppermute | solution.py:41
  161.1 25.7 %collective-permute-start.17 = (bf16[64,4096]{1,0:T(8,128)(2,1)S(1)}, bf16[64,4096]{1,0:T(8,128)(2,1)}, u32[]{:S(2)}, u32[]{:S(2)}) collective-permute-start(bf16[64,4096]{1,0:T(8,128)(2,1)S(1)} %pad_maximum_fusion.2.a0), channel_id=1, source_target_pairs={{0,64},{16,80},{32,96},{48,112},{64,0},{80,16},{96,32},{112,48},{1... | collective-permute-start | bytes 1572872 | tf_op jit(solution)/shard_map/route/ppermute | solution.py:41
  163.5 24.0 %collective-permute-start.18 = (bf16[64,4096]{1,0:T(8,128)(2,1)S(1)}, bf16[64,4096]{1,0:T(8,128)(2,1)}, u32[]{:S(2)}, u32[]{:S(2)}) collective-permute-start(bf16[64,4096]{1,0:T(8,128)(2,1)S(1)} %pad_maximum_fusion.2.a0), channel_id=1, source_target_pairs={{0,96},{16,112},{32,0},{48,16},{64,32},{80,48},{96,64},{112,80},{1... | collective-permute-start | bytes 1572872 | tf_op jit(solution)/shard_map/route/ppermute | solution.py:41
  (6 other events, 20.8 us)
Sparse Core Ops, SparseCore 0:
  12.6 148.0 all-gather.2
  197.8 33.5 all-gather.4
where the time goes:
time: 297 us; the launch traced here: 300 us
  Pallas kernels  116 us (39%)
  waiting for transfers between devices  113 us (38%)
  starting transfers between devices  39.8 us (13%)
  between operations  15.5 us (5%)
  other arithmetic  8.42 us (3%)
  local copies, waits for them, and re-layouts  7.42 us (2%)
    ppermute x15, waiting for transfers between devices, seq_shift(): return lax.ppermute(array, 'seq', pairs)  65.5 us
    pallas_call x1, Pallas kernels, attend(): pl.pallas_call(attention_kernel, in_specs=[pl.BlockSpec(memory_space=pltp...  62 us
    ppermute x8, waiting for transfers between devices, pool_shift(): return lax.ppermute(array, 'pool', pairs)  23.3 us
    pallas_call x1, Pallas kernels, query(): pl.pallas_call(query_kernel, grid=(width // CHUNK,), in_specs=[pl.BlockSp...  19.7 us
    ppermute x15, starting transfers between devices, seq_shift(): return lax.ppermute(array, 'seq', pairs)  17.3 us
    ppermute x8, starting transfers between devices, pool_shift(): return lax.ppermute(array, 'pool', pairs)  16 us
    all_gather x1, waiting for transfers between devices, per_device(): kv_all = lax.all_gather(kv, 'seq', axis=0, tiled=True)  14 us
    pallas_call x1, Pallas kernels, merger(): pl.pallas_call(merger_kernel, grid=(width // block,), in_specs=[whole(pie...  13.7 us
  transfers between devices with their start and end apart: 26, of which 18 were waited for; matrix products, arithmetic and copies ran while one was open for 4% of the time, Pallas kernels for 14%

commit v1 on v0

--- a/solution.py
+++ b/solution.py
@@ -16,6 +16,8 @@
 X, Y, C = 4, 2, 2
 Z, YH = 4, 2
 CHUNK = 1024
+SLOT_CHUNK = 4096
+SEQ, POOL = "seq", "pool"
 
 
 def rms_rows(matrix):
@@ -27,10 +29,11 @@
     for source in range(X * Y * C):
         x, y, c = source // (Y * C), source // C % Y, source % C
         pairs.append((source, ((x + dx) % X) * Y * C + (y ^ dy) * C + (c ^ dc)))
-    return lax.ppermute(array, "seq", pairs)
-
-
-HALF_D = 4096
+    return lax.ppermute(array, SEQ, pairs)
+
+
+SUM_SPLIT = 4096
+POOL_SPLIT = 4096
 
 
 def pool_shift(array, dz, dy):
@@ -38,7 +41,7 @@
     for source in range(Z * YH):
         z, y = source // YH, source % YH
         pairs.append((source, ((z + dz) % Z) * YH + (y ^ dy)))
-    return lax.ppermute(array, "pool", pairs)
+    return lax.ppermute(array, POOL, pairs)
 
 
 def whole(shape):
@@ -76,59 +79,72 @@
     )(patches, segment[None, :])
 
 
+ANY = pl.BlockSpec(memory_space=pl.ANY)
+VMEM = pl.BlockSpec(memory_space=pltpu.VMEM)
+SMEM = pl.BlockSpec(memory_space=pltpu.SMEM)
+
+
 def merger_kernel(*refs):
-    pieces, (up_a, up_b, down_a, down_b), outs = refs[:X], refs[X:X + 4], refs[X + 4:X + 4 + X + Y]
-    hidden_ref = refs[-1]
-    rows = pieces[0].shape[0]
-    depth = up_a.shape[1]
-    step = pl.program_id(0)
-    half = pl.num_programs(0) // 2
-
-    @pl.when(step == 0)
-    def _():
-        merged = jnp.concatenate([piece[:, :depth] for piece in pieces], axis=0)
-        up = jnp.concatenate([up_a[...], up_b[...]], axis=0)
-        value = lax.dot_general(merged, up, (((1,), (1,)), ((), ())), preferred_element_type=jnp.float32)
-        value = 0.5 * value * (1.0 + lax.erf(value * (0.5 ** 0.5)))
-        hidden_ref[...] = value.astype(jnp.bfloat16)
-
-    down = jnp.concatenate([down_a[...], down_b[...]], axis=0)
-    total = jnp.dot(hidden_ref[...], down, preferred_element_type=jnp.float32)
-
-    @pl.when(step < half)
-    def _():
-        for dx in range(X):
-            outs[dx][...] = total[dx * rows:(dx + 1) * rows].astype(outs[dx].dtype)
-
-    @pl.when(step >= half)
-    def _():
-        own = rows // Y
-        for dx in range(X):
-            for dy in range(Y):
-                at = dx * rows + dy * own
-                outs[X + dy][dx * own:(dx + 1) * own, :] = total[at:at + own].astype(outs[X + dy].dtype)
+    pieces, (up_a, up_b, down_a, down_b), refs = refs[:X], refs[X:X + 4], refs[X + 4:]
+    outs, (up_ref, down_ref, sems) = refs[:X + Y], refs[X + Y:]
+    units, depth = up_a.shape
+    own = pieces[0].shape[0] // Y
+    halves = [slice(0, SUM_SPLIT), slice(SUM_SPLIT, down_a.shape[1])]
+    copies = []
+    for at, source in enumerate((up_a, up_b)):
+        copies.append(pltpu.make_async_copy(source, up_ref.at[pl.ds(at * units, units), :], sems.at[at]))
+    for n, half in enumerate(halves):
+        for at, source in enumerate((down_a, down_b)):
+            copies.append(
+                pltpu.make_async_copy(
+                    source.at[:, half], down_ref.at[pl.ds(at * units, units), half], sems.at[2 + 2 * n + at]
+                )
+            )
+    for copy in copies:
+        copy.start()
+    merged = jnp.concatenate([piece[:, :depth] for piece in pieces], axis=0)
+    hidden = []
+    for at in range(2):
+        copies[at].wait()
+        value = lax.dot_general(
+            merged, up_ref[at * units:(at + 1) * units, :], (((1,), (1,)), ((), ())),
+            preferred_element_type=jnp.float32,
+        )
+        hidden.append((0.5 * value * (1.0 + lax.erf(value * (0.5 ** 0.5)))).astype(jnp.bfloat16))
+    hidden = jnp.concatenate(hidden, axis=1)
+    for n, half in enumerate(halves):
+        copies[2 + 2 * n].wait()
+        copies[3 + 2 * n].wait()
+        for start in range(half.start, half.stop, CHUNK):
+            total = jnp.dot(hidden, down_ref[:, start:start + CHUNK], preferred_element_type=jnp.float32)
+            part = slice(start - half.start, start - half.start + CHUNK)
+            if n == 0:
+                for dx in range(X):
+                    at = dx * Y * own
+                    outs[dx][:, part] = total[at:at + Y * own].astype(outs[dx].dtype)
+            else:
+                for dx in range(X):
+                    for dy in range(Y):
+                        at = (dx * Y + dy) * own
+                        outs[X + dy][dx * own:(dx + 1) * own, part] = total[at:at + own].astype(outs[X + dy].dtype)
 
 
 def merger(pieces, ups, downs):
-    rows = pieces[0].shape[0]
     units, depth = ups[0].shape
     width = downs[0].shape[1]
-    block = 1024
-    half = HALF_D // block
-    first = lambda shape: pl.BlockSpec(shape, lambda n: (0, jnp.minimum(n, half - 1)))
-    second = lambda shape: pl.BlockSpec(shape, lambda n: (0, jnp.maximum(n - half, 0)))
-    own = rows // Y
+    own = pieces[0].shape[0] // Y
     shape = jax.ShapeDtypeStruct
     return pl.pallas_call(
         merger_kernel,
-        grid=(width // block,),
-        in_specs=[whole(pieces[0].shape)] * X
-        + [whole((units, depth))] * 2
-        + [pl.BlockSpec((units, block), lambda n: (0, n))] * 2,
-        out_specs=[first((rows, block))] * X + [second((X * own, block))] * Y,
-        out_shape=[shape((rows, HALF_D), jnp.float32 if dx == 0 else jnp.bfloat16) for dx in range(X)]
-        + [shape((X * own, width - HALF_D), jnp.float32 if dy == 0 else jnp.bfloat16) for dy in range(Y)],
-        scratch_shapes=[pltpu.VMEM((X * rows, 2 * units), jnp.bfloat16)],
+        in_specs=[VMEM] * X + [ANY] * 4,
+        out_specs=[VMEM] * (X + Y),
+        out_shape=[shape((Y * own, SUM_SPLIT), jnp.float32 if dx == 0 else jnp.bfloat16) for dx in range(X)]
+        + [shape((X * own, width - SUM_SPLIT), jnp.float32 if dy == 0 else jnp.bfloat16) for dy in range(Y)],
+        scratch_shapes=[
+            pltpu.VMEM((2 * units, depth), jnp.bfloat16),
+            pltpu.VMEM((2 * units, width), jnp.bfloat16),
+            pltpu.SemaphoreType.DMA((6,)),
+        ],
         compiler_params=pltpu.CompilerParams(vmem_limit_bytes=VMEM_BYTES),
         name="merger",
     )(*pieces, *ups, *downs)
@@ -161,6 +177,14 @@
     for at in range(HD, matrix.shape[1], HD):
         total += matrix[:, at:at + HD]
     return total
+
+
+KV_BLOCK = 4
+
+
+def slot_columns(refs, n, chunk):
+    part = pl.ds(pl.multiple_of(n * chunk, chunk), chunk)
+    return jnp.concatenate([ref[:, part] for ref in refs], axis=0)
 
 
 def text_kernel(text_ref, weight_ref, kv_ref, total_ref):
@@ -199,8 +223,8 @@
     rows = text_kv_ref.shape[0]
     step = pl.program_id(0)
     steps = pl.num_programs(0)
-    half = HALF_D // CHUNK
-    width = steps * CHUNK
+    half = POOL_SPLIT // SLOT_CHUNK
+    width = steps * SLOT_CHUNK
 
     @pl.when(step == 0)
     def _():
@@ -208,8 +232,7 @@
         total_ref[...] = jnp.zeros_like(total_ref)
 
     def add(at, refs, index):
-        part = pl.ds(pl.multiple_of(index * CHUNK, CHUNK), CHUNK)
-        slots = jnp.concatenate([ref[:, part] for ref in refs], axis=0)
+        slots = slot_columns(refs, index, SLOT_CHUNK)
         sum_ref[at] += jnp.dot(slots, weight_ref[...], preferred_element_type=jnp.float32)
         value = slots.astype(jnp.float32)
         total_ref[at] += lane_sums(value * value)
@@ -263,10 +286,10 @@
     shape = jax.ShapeDtypeStruct
     return pl.pallas_call(
         slot_kernel,
-        grid=(width // CHUNK,),
+        grid=(width // SLOT_CHUNK,),
         in_specs=[whole(piece.shape) for piece in slots_a]
         + [whole(piece.shape) for piece in slots_b]
-        + [pl.BlockSpec((CHUNK, 2 * HD), lambda n: (n, kv_block))]
+        + [pl.BlockSpec((SLOT_CHUNK, 2 * HD), lambda n: (n, kv_block))]
         + [whole((rows, 2 * HD)), whole((rows, HD)), whole((rows, HD)), whole((rows, HD))],
         out_specs=[whole((rows, 2 * HD)), whole((rows, HD))],
         out_shape=[shape((rows, 2 * HD), jnp.bfloat16), shape((rows, HD), jnp.float32)],
@@ -282,6 +305,7 @@
 GROUP = 2
 SOFT = HD ** (-0.5) * LOG2E
 LIMIT = 60.0
+STEP = 4
 
 
 def query_kernel(
@@ -291,7 +315,7 @@
     rows = text_ref.shape[0]
     step = pl.program_id(0)
     steps = pl.num_programs(0)
-    half = HALF_D // CHUNK
+    half = POOL_SPLIT // CHUNK
     wide = GROUP * rows
 
     @pl.when(step == 0)
@@ -303,8 +327,7 @@
         total_ref[...] = jnp.zeros_like(total_ref)
 
     def add(pick, refs, index):
-        part = pl.ds(pl.multiple_of(index * CHUNK, CHUNK), CHUNK)
-        slots = jnp.concatenate([ref[:, part] for ref in refs], axis=0)
+        slots = slot_columns(refs, index, CHUNK)
         image = jnp.dot(pick[...], slots, preferred_element_type=jnp.float32)
         mixed = jnp.where(held_ref[:, 2:3] > 0.5, image, text_ref[...].astype(jnp.float32)).astype(jnp.bfloat16)
         total_ref[...] += jnp.dot(mixed, weight_ref[...], preferred_element_type=jnp.float32)
@@ -383,7 +406,7 @@
     wide = GROUP * rows
     me = info_ref[0]
     first = info_ref[1]
-    edge = info_ref[2]
+    clear = info_ref[2]
     count = me - first
 
     def allowed_keys(indices):
@@ -439,31 +462,31 @@
         sum_ref[...] = sum_in[...]
         acc_ref[...] = acc_in[...]
 
-    def either(indices):
-        needs = indices[-1] * rows < edge
-
-        @pl.when(needs)
-        def _():
-            fast(indices, True)
-
-        @pl.when(jnp.logical_not(needs))
-        def _():
-            fast(indices, False)
-
     start()
     base_ref[...] = top_in[...] * SOFT
-    odd = count % 2
-
-    @pl.when(odd == 1)
-    def _():
-        either([me - 1])
-
-    def pair(i, _):
-        at = me - 1 - odd - 2 * i
-        either([at, at - 1])
+    plain = me - clear
+
+    def step(i, _):
+        at = me - 1 - STEP * i
+        fast([at - n for n in range(STEP)], False)
         return 0
 
-    lax.fori_loop(0, count // 2, pair, 0)
+    lax.fori_loop(0, plain // STEP, step, 0)
+    left = plain % STEP
+
+    @pl.when(left >= 2)
+    def _():
+        fast([clear + left - 1, clear + left - 2], False)
+
+    @pl.when(left % 2 == 1)
+    def _():
+        fast([clear], False)
+
+    def masked_step(i, _):
+        fast([clear - 1 - i], True)
+        return 0
+
+    lax.fori_loop(0, clear - first, masked_step, 0)
     grown = jnp.max(top_ref[...] * SOFT - base_ref[...])
 
     @pl.when(grown > LIMIT)
@@ -512,24 +535,25 @@
     key_weight,
     value_weight,
 ):
-    seq_count = lax.axis_size("seq")
-    seq_index = lax.axis_index("seq")
+    seq_count = lax.axis_size(SEQ)
+    seq_index = lax.axis_index(SEQ)
     rows, width = text_rows.shape
     bf16, f32 = jnp.bfloat16, jnp.float32
 
+    def after(array, *others):
+        return lax.optimization_barrier((array, *others))[0]
+
     with jax.named_scope("merger"):
+        merged = prepare(patches, segment)
+        own = merged.shape[0]
+        merged_beside = seq_shift(merged, 0, 1, 0)
+        own_weights = jnp.concatenate(
+            after((query_weight, key_weight, value_weight), merged_beside), axis=1
+        )
+        weights = lax.all_gather(own_weights, SEQ, axis=0, tiled=True)
         up_other = seq_shift(merge_up.T, 0, 0, 1)
         down_other = seq_shift(merge_down, 0, 0, 1)
-        merged = prepare(patches, segment)
-        own = merged.shape[0]
-        beside = seq_shift(merged, 0, 1, 0)
-        merged, query_weight, key_weight, value_weight = lax.optimization_barrier(
-            (merged, query_weight, key_weight, value_weight)
-        )
-        weights = lax.all_gather(
-            jnp.concatenate([query_weight, key_weight, value_weight], axis=1), "seq", axis=0, tiled=True
-        )
-        pair = jnp.concatenate([merged, beside], axis=0)
+        pair = jnp.concatenate([merged, merged_beside], axis=0)
         pieces = [pair] + [seq_shift(pair, dx, 0, 0) for dx in range(1, X)]
         outs = merger(pieces, (merge_up.T, up_other), (merge_down, down_other))
         part_a, part_b = outs[:X], outs[X:]
@@ -546,7 +570,9 @@
 
     with jax.named_scope("segments"):
         counted = sum(
-            piece[at:at + 1, merge_up.shape[0]:].astype(f32) for piece in pieces for at in range(0, Y * own, own)
+            block[at:at + 1, merge_up.shape[0]:].astype(f32)
+            for block in pieces
+            for at in range(0, Y * own, own)
         )
         counted = (counted + seq_shift(counted, 0, 0, 1))[0]
         ends = (counted[:3] * 128.0 + counted[3:6]).astype(jnp.int32)
@@ -554,7 +580,8 @@
         starts = jnp.sum(
             jnp.where(segment[None, :] == jnp.arange(4, dtype=jnp.int32)[:, None], before[:, None], 0), axis=0
         )
-        info = jnp.stack([seq_index, starts[0] // rows, starts[-1]]).astype(jnp.int32)
+        clear = jnp.minimum((starts[-1] + rows - 1) // rows, seq_index)
+        info = jnp.stack([seq_index, starts[0] // rows, clear]).astype(jnp.int32)
         starts = (starts - seq_index * rows)[None, :]
 
     with jax.named_scope("angles"):
@@ -578,19 +605,20 @@
             select, jnp.concatenate([image_a, image_b, marks], axis=1), preferred_element_type=f32
         ).astype(bf16)
         got = lax.all_to_all(
-            send.reshape(seq_count, CAP, width + AUX), "seq", split_axis=0, concat_axis=0, tiled=True
+            send.reshape(seq_count, CAP, width + AUX), SEQ, split_axis=0, concat_axis=0, tiled=True
         ).reshape(seq_count * CAP, width + AUX)
         got, info, starts, cosine, sine = lax.optimization_barrier((got, info, starts, cosine, sine))
-        got_a, got_b = got[:, :HALF_D], got[:, HALF_D:]
+        got_a, got_b = got[:, :POOL_SPLIT], got[:, POOL_SPLIT:]
         pair_a = jnp.concatenate([got_a, pool_shift(got_a, 0, 1)], axis=0)
         column_b = jnp.concatenate([got_b] + [pool_shift(got_b, dz, 0) for dz in range(1, Z)], axis=0)
+        pair_a, column_b, text_here = lax.optimization_barrier((pair_a, column_b, text_rows))
         slots_a = [pair_a] + [pool_shift(pair_a, dz, 0) for dz in range(1, Z)]
         slots_b = [column_b, pool_shift(column_b, 0, 1)]
 
     with jax.named_scope("project"):
-        text_kv, text_total = project_text(text_rows, weights)
+        text_kv, text_total = project_text(text_here, weights)
         kv, scale = project_slots(slots_a, slots_b, weights, text_kv, text_total, cosine, sine)
-        kv_all = lax.all_gather(kv, "seq", axis=0, tiled=True)
+        kv_all = lax.all_gather(kv, SEQ, axis=0, tiled=True)
         state = query(
             text_rows, slots_a, slots_b, weights, scale, cosine, sine, kv, starts, query_weight.shape[1] // HD
         )

time: 297 us -> 284 us (0.956)
  the two profiles are of different devices: /device:TPU:6 before, /device:TPU:95 now
where the time goes in v1:
time: 284 us; the launch traced here: 283 us
  waiting for transfers between devices  115 us (40%)
  Pallas kernels  101 us (36%)
  starting transfers between devices  37.2 us (13%)
  between operations  16.4 us (6%)
  other arithmetic  8.55 us (3%)
  local copies, waits for them, and re-layouts  5.13 us (2%)
    ppermute x15, waiting for transfers between devices, seq_shift(): return lax.ppermute(array, SEQ, pairs)  59.9 us
    pallas_call x1, Pallas kernels, attend(): pl.pallas_call(attention_kernel, in_specs=[pl.BlockSpec(memory_space=pltp...  54 us
    pallas_call x1, Pallas kernels, query(): pl.pallas_call(query_kernel, grid=(width // CHUNK,), in_specs=[pl.BlockSp...  19.8 us
    ppermute x8, waiting for transfers between devices, pool_shift(): return lax.ppermute(array, POOL, pairs)  19 us
    ppermute x15, starting transfers between devices, seq_shift(): return lax.ppermute(array, SEQ, pairs)  16.5 us
    all_gather x1, waiting for transfers between devices, per_device(): kv_all = lax.all_gather(kv, SEQ, axis=0, tiled=True)  15.8 us
    all_gather x1, waiting for transfers between devices, per_device(): weights = lax.all_gather(own_weights, SEQ, axis=0, tiled=True)  12.6 us
    ppermute x8, starting transfers between devices, pool_shift(): return lax.ppermute(array, POOL, pairs)  11.2 us
  transfers between devices with their start and end apart: 26, of which 18 were waited for; matrix products, arithmetic and copies ran while one was open for 3% of the time, Pallas kernels for 14%

profile of v1, /device:TPU:95, one launch (start us, length us, event | category | flops | bytes accessed | tf_op | source)
XLA Modules:
  0.0 283.3 jit_solution(1633225533929531533)
XLA Ops:
  7.9 1.9 prepare.1
  10.3 5.0 %collective-permute-done = bf16[16,5248]{1,0:T(8,128)(2,1)} collective-permute-done((bf16[16,5248]{1,0:T(8,128)(2,1)}, bf16[16,5248]{1,0:T(8,128)(2,1)}, u32[]{:S(2)}, u32[]{:S(2)}) %collective-permute-start) | collective-permute-done | bytes 167968 | tf_op jit(solution)/shard_map/merger/ppermute | solution.py:32
  15.3 2.5 pad_maximum_fusion
  17.9 1.6 collective-permute-start.5
  21.3 2.1 collective-permute-start.2
  24.3 5.9 %collective-permute-done.1.refs_1_ = bf16[32,5248]{1,0:T(8,128)(2,1)S(1)} collective-permute-done((bf16[32,5248]{1,0:T(8,128)(2,1)S(1)}, bf16[32,5248]{1,0:T(8,128)(2,1)S(1)}, u32[]{:S(2)}, u32[]{:S(2)}) %collective-permute-start.1) | collective-permute-done | bytes 335904 | tf_op jit(solution)/shard_map/merger/ppermute | solution.py:32
  31.6 13.2 %collective-permute-done.3.refs_3_ = bf16[32,5248]{1,0:T(8,128)(2,1)S(1)} collective-permute-done((bf16[32,5248]{1,0:T(8,128)(2,1)S(1)}, bf16[32,5248]{1,0:T(8,128)(2,1)S(1)}, u32[]{:S(2)}, u32[]{:S(2)}) %collective-permute-start.3) | collective-permute-done | bytes 335904 | tf_op jit(solution)/shard_map/merger/ppermute | solution.py:32
  45.6 3.8 %collective-permute-start.14 = (f32[1,128]{1,0:T(1,128)S(1)}, f32[1,128]{1,0:T(1,128)S(1)}, u32[]{:S(2)}, u32[]{:S(2)}) collective-permute-start(f32[1,128]{1,0:T(1,128)S(1)} %fusion.16), channel_id=1, source_target_pairs={{0,1},{1,0},{2,3},{3,2},{4,5},{5,4},{6,7},{7,6},{8,9},{9,8},{10,11... | collective-permute-start | bytes 1544 | tf_op jit(solution)/shard_map/segments/ppermute | solution.py:32
  50.4 9.8 %merger.1 = (f32[32,4096]{1,0:T(8,128)}, bf16[32,4096]{1,0:T(8,128)(2,1)}, bf16[32,4096]{1,0:T(8,128)(2,1)}, bf16[32,4096]{1,0:T(8,128)(2,1)}, f32[64,4096]{1,0:T(8,128)}, /*index=5*/bf16[64,4096]{1,0:T(8,128)(2,1)}) custom-call(bf16[32,5248]{1,0:T(8,128)(2,1)} %copy-done.5, bf16[32,5248]{1,0:T(8,128)(2,1)} %copy-done.8, bf16[32,5248]{1,0:T(8,128)(2,1)} %copy-done.9, ...), custom_call_target="tpu_custom_call" | custom-call | tf_op jit(solution)/shard_map/merger/merger/pallas_call | solution.py:137
  61.8 2.5 collective-permute-start.7
  64.7 10.4 %collective-permute-done.8 = bf16[32,4096]{1,0:T(8,128)(2,1)S(1)} collective-permute-done((bf16[32,4096]{1,0:T(8,128)(2,1)}, bf16[32,4096]{1,0:T(8,128)(2,1)S(1)}, u32[]{:S(2)}, u32[]{:S(2)}) %collective-permute-start.8) | collective-permute-done | bytes 262176 | tf_op jit(solution)/shard_map/sums/ppermute | solution.py:32
  75.2 2.1 collective-permute-done.7
  77.2 10.1 %collective-permute-done.6 = bf16[32,4096]{1,0:T(8,128)(2,1)S(1)} collective-permute-done((bf16[32,4096]{1,0:T(8,128)(2,1)}, bf16[32,4096]{1,0:T(8,128)(2,1)S(1)}, u32[]{:S(2)}, u32[]{:S(2)}) %collective-permute-start.6) | collective-permute-done | bytes 262176 | tf_op jit(solution)/shard_map/sums/ppermute | solution.py:32
  90.6 2.4 collective-permute-start.12
  93.1 3.3 %collective-permute-done.9 = bf16[16,4096]{1,0:T(8,128)(2,1)S(1)} collective-permute-done((bf16[16,4096]{1,0:T(8,128)(2,1)S(1)}, bf16[16,4096]{1,0:T(8,128)(2,1)S(1)}, u32[]{:S(2)}, u32[]{:S(2)}) %collective-permute-start.9) | collective-permute-done | bytes 131104 | tf_op jit(solution)/shard_map/sums/ppermute | solution.py:32
  97.6 1.9 collective-permute-done.12
  99.5 4.6 %collective-permute-done.11 = bf16[16,4096]{1,0:T(8,128)(2,1)S(1)} collective-permute-done((bf16[16,4096]{1,0:T(8,128)(2,1)S(1)}, bf16[16,4096]{1,0:T(8,128)(2,1)S(1)}, u32[]{:S(2)}, u32[]{:S(2)}) %collective-permute-start.11) | collective-permute-done | bytes 131104 | tf_op jit(solution)/shard_map/sums/ppermute | solution.py:32
  105.4 9.5 %all-to-all-start = ((bf16[16,2,8320]{2,1,0:T(2,128)(2,1)}), bf16[16,2,8320]{2,1,0:T(2,128)(2,1)S(1)}, u32[]{:S(2)}, u32[]{:S(2)}) async-start(bf16[16,2,8320]{2,1,0:T(2,128)(2,1)} %reshape.61), calls=%async_computation | async-start | bytes 1064960 | tf_op jit(solution)/shard_map/route/all_to_all | solution.py:607
  119.6 7.3 %all-to-all-done = bf16[16,2,8320]{2,1,0:T(2,128)(2,1)S(1)} async-done(((bf16[16,2,8320]{2,1,0:T(2,128)(2,1)}), bf16[16,2,8320]{2,1,0:T(2,128)(2,1)S(1)}, u32[]{:S(2)}, u32[]{:S(2)}) %all-to-all-start) | async-done | bytes 532512 | tf_op jit(solution)/shard_map/route/all_to_all | solution.py:607
  128.2 3.6 %collective-permute-start.17 = (bf16[32,4224]{1,0:T(8,128)(2,1)S(1)}, bf16[32,4224]{1,0:T(8,128)(2,1)S(1)}, u32[]{:S(2)}, u32[]{:S(2)}) collective-permute-start(bf16[32,4224]{1,0:T(8,128)(2,1)S(1)} %slice.85), channel_id=1, source_target_pairs={{0,64},{16,80},{32,96},{48,112},{64,0},{80,16},{96,32},{112,48},{1... | collective-permute-start | bytes 811016 | tf_op jit(solution)/shard_map/route/ppermute | solution.py:44
  131.8 10.4 %collective-permute-done.15 = bf16[32,4096]{1,0:T(8,128)(2,1)S(1)} collective-permute-done((bf16[32,4096]{1,0:T(8,128)(2,1)S(1)}, bf16[32,4096]{1,0:T(8,128)(2,1)S(1)}, u32[]{:S(2)}, u32[]{:S(2)}) %collective-permute-start.15) | collective-permute-done | bytes 262176 | tf_op jit(solution)/shard_map/route/ppermute | solution.py:44
  142.2 2.4 collective-permute-done.16
  144.7 2.3 collective-permute-start.22
  147.0 2.2 collective-permute-start.20
  149.2 2.1 collective-permute-start.21
  151.3 12.6 %all-gather.3.cloned.1.call-done.weight_ref = bf16[8192,1280]{1,0:T(8,128)(2,1)} async-done(((bf16[512,1280]{1,0:T(8,128)(2,1)}), bf16[8192,1280]{1,0:T(8,128)(2,1)}) %all-gather.3.cloned.1.call-update) | async-done | bytes 20971536 | tf_op jit(solution)/shard_map/merger/all_gather | solution.py:553
  163.9 9.4 %project_text.1 = (f32[384,256]{1,0:T(8,128)}, f32[384,128]{1,0:T(8,128)}) custom-call(bf16[384,8192]{1,0:T(8,128)(2,1)} %text_ref.2, bf16[8192,1280]{1,0:T(8,128)(2,1)} %all-gather.3.cloned.1.call-done.weight_ref), custom_call_target="tpu_custom_call" | custom-call | tf_op jit(solution)/shard_map/project/project_text/pallas_call | solution.py:205
  173.4 6.3 %collective-permute-done.22.b1 = bf16[128,4224]{1,0:T(8,128)(2,1)S(1)} collective-permute-done((bf16[128,4224]{1,0:T(8,128)(2,1)S(1)}, bf16[128,4224]{1,0:T(8,128)(2,1)S(1)}, u32[]{:S(2)}, u32[]{:S(2)}) %collective-permute-start.22) | collective-permute-done | bytes 1081376 | tf_op jit(solution)/shard_map/route/ppermute | solution.py:44
  180.7 6.1 %project_slots.1 = (bf16[384,256]{1,0:T(8,128)(2,1)}, f32[384,128]{1,0:T(8,128)}) custom-call(bf16[64,4096]{1,0:T(8,128)(2,1)} %copy-done.1, bf16[64,4096]{1,0:T(8,128)(2,1)} %copy-done.4, bf16[64,4096]{1,0:T(8,128)(2,1)} %collective-permute-done.20.a2, bf16[64,4096]{1,0:T(8,128)(2,1)} %collective-permute-done.21.a3, bf16[128,4224]{1,0:T(8,128)(2,1)} %copy-done, ...), custom_call_target="tpu_custom_call" | custom-call | tf_op jit(solution)/shard_map/project/project_slots/pallas_call | solution.py:287
  186.8 19.8 %query.1 = (bf16[3072,128]{1,0:T(8,128)(2,1)}, f32[1,3072]{1,0:T(1,128)}, f32[1,3072]{1,0:T(1,128)}, f32[128,3072]{1,0:T(8,128)}) custom-call(bf16[384,8192]{1,0:T(8,128)(2,1)} %text_ref.2, bf16[64,4096]{1,0:T(8,128)(2,1)} %copy-done.1, bf16[64,4096]{1,0:T(8,128)(2,1)} %copy-done.4, bf16[64,4096]{1,0:T(8,128)(2,1)} %collective-permute-done.20.a2, ...), custom_call_target="tpu_custom_call" | custom-call | tf_op jit(solution)/shard_map/project/query/pallas_call | solution.py:374
  206.7 15.8 %all-gather.5.cloned.1.call-done = bf16[6144,256]{1,0:T(8,128)(2,1)} async-done(((bf16[384,256]{1,0:T(8,128)(2,1)}), bf16[6144,256]{1,0:T(8,128)(2,1)}) %all-gather.5.cloned.1.call-update) | async-done | bytes 3145744 | tf_op jit(solution)/shard_map/project/all_gather | solution.py:621
  222.4 54.0 %attend.1 = bf16[384,1024]{1,0:T(8,128)(2,1)} custom-call(s32[3]{0:T(128)} %pad_add_fusion.1.info_ref, bf16[3072,128]{1,0:T(8,128)(2,1)} %get-tuple-element.51.q_ref, f32[1,3072]{1,0:T(1,128)} %get-tuple-element.52.top_in, f32[1,3072]{1,0:T(1,128)} %get-tuple-element.53.sum_in, f32[128,3072]{1,0:T(8,128)} %get-tuple-element.54.acc_in, ...), custom_call_target="tpu_custom_call" | custom-call | tf_op jit(solution)/shard_map/attend/attend/pallas_call | solution.py:511
  (92 shorter events, 19.9 us)
Async XLA Ops:
  6.5 157.4 %all-gather.3.cloned.1.call-start = ((), (), s32[]{:S(2)}) async-start(), calls=%async_computation.1 | async-start | bytes 22282240 | tf_op jit(solution)/shard_map/merger/all_gather | solution.py:553
  9.9 5.5 %collective-permute-start = (bf16[16,5248]{1,0:T(8,128)(2,1)}, bf16[16,5248]{1,0:T(8,128)(2,1)}, u32[]{:S(2)}, u32[]{:S(2)}) collective-permute-start(bf16[16,5248]{1,0:T(8,128)(2,1)} %prepare.1), channel_id=1, source_target_pairs={{0,2},{1,3},{2,0},{3,1},{4,6},{5,7},{6,4},{7,5},{8,10},{9,11},{10,... | collective-permute-start | bytes 503816 | tf_op jit(solution)/shard_map/merger/ppermute | solution.py:32
  17.9 32.5 %collective-permute-start.5 = (bf16[320,8192]{1,0:T(8,128)(2,1)}, bf16[320,8192]{1,0:T(8,128)(2,1)}, u32[]{:S(2)}, u32[]{:S(2)}) collective-permute-start(bf16[320,8192]{1,0:T(8,128)(2,1)} %refs_6_.1), channel_id=1, source_target_pairs={{0,1},{1,0},{2,3},{3,2},{4,5},{5,4},{6,7},{7,6},{8,9},{9,8},{10,11... | collective-permute-start | bytes 15728648 | tf_op jit(solution)/shard_map/merger/ppermute | solution.py:32
  19.5 30.9 %collective-permute-start.4 = (bf16[320,5120]{1,0:T(8,128)(2,1)S(1)}, bf16[320,5120]{1,0:T(8,128)(2,1)}, u32[]{:S(2)}, u32[]{:S(2)}) collective-permute-start(bf16[320,5120]{1,0:T(8,128)(2,1)S(1)} %bitcast.17), channel_id=1, source_target_pairs={{0,1},{1,0},{2,3},{3,2},{4,5},{5,4},{6,7},{7,6},{8,9},{9,8},{10,11... | collective-permute-start | bytes 9830408 | tf_op jit(solution)/shard_map/merger/ppermute | solution.py:32
  21.1 9.1 %collective-permute-start.1 = (bf16[32,5248]{1,0:T(8,128)(2,1)S(1)}, bf16[32,5248]{1,0:T(8,128)(2,1)S(1)}, u32[]{:S(2)}, u32[]{:S(2)}) collective-permute-start(bf16[32,5248]{1,0:T(8,128)(2,1)S(1)} %pad_maximum_fusion.3.refs_0_), channel_id=1, source_target_pairs={{0,4},{1,5},{2,6},{3,7},{4,8},{5,9},{6,10},{7,11},{8,12},{9,13},{1... | collective-permute-start | bytes 1007624 | tf_op jit(solution)/shard_map/merger/ppermute | solution.py:32
  21.3 10.3 %collective-permute-start.2 = (bf16[32,5248]{1,0:T(8,128)(2,1)S(1)}, bf16[32,5248]{1,0:T(8,128)(2,1)S(1)}, u32[]{:S(2)}, u32[]{:S(2)}) collective-permute-start(bf16[32,5248]{1,0:T(8,128)(2,1)S(1)} %pad_maximum_fusion.3.refs_0_), channel_id=1, source_target_pairs={{0,8},{1,9},{2,10},{3,11},{4,12},{5,13},{6,14},{7,15},{8,0},{9,1},... | collective-permute-start | bytes 1007624 | tf_op jit(solution)/shard_map/merger/ppermute | solution.py:32
  23.5 21.4 %collective-permute-start.3 = (bf16[32,5248]{1,0:T(8,128)(2,1)S(1)}, bf16[32,5248]{1,0:T(8,128)(2,1)S(1)}, u32[]{:S(2)}, u32[]{:S(2)}) collective-permute-start(bf16[32,5248]{1,0:T(8,128)(2,1)S(1)} %pad_maximum_fusion.3.refs_0_), channel_id=1, source_target_pairs={{0,12},{1,13},{2,14},{3,15},{4,0},{5,1},{6,2},{7,3},{8,4},{9,5},{1... | collective-permute-start | bytes 1007624 | tf_op jit(solution)/shard_map/merger/ppermute | solution.py:32
  30.2 15.4 %copy-start.8 = (bf16[32,5248]{1,0:T(8,128)(2,1)}, bf16[32,5248]{1,0:T(8,128)(2,1)S(1)}, u32[]{:S(2)}) copy-start(bf16[32,5248]{1,0:T(8,128)(2,1)S(1)} %collective-permute-done.1.refs_1_) | copy-start | bytes 1007620
  31.6 17.8 %copy-start.9 = (bf16[32,5248]{1,0:T(8,128)(2,1)}, bf16[32,5248]{1,0:T(8,128)(2,1)S(1)}, u32[]{:S(2)}) copy-start(bf16[32,5248]{1,0:T(8,128)(2,1)S(1)} %collective-permute-done.2.refs_2_) | copy-start | bytes 1007620
  45.6 4.8 %collective-permute-start.14 = (f32[1,128]{1,0:T(1,128)S(1)}, f32[1,128]{1,0:T(1,128)S(1)}, u32[]{:S(2)}, u32[]{:S(2)}) collective-permute-start(f32[1,128]{1,0:T(1,128)S(1)} %fusion.16), channel_id=1, source_target_pairs={{0,1},{1,0},{2,3},{3,2},{4,5},{5,4},{6,7},{7,6},{8,9},{9,8},{10,11... | collective-permute-start | bytes 1544 | tf_op jit(solution)/shard_map/segments/ppermute | solution.py:32
  60.2 29.4 %copy-start.6 = (f32[64,4096]{1,0:T(8,128)S(1)}, f32[64,4096]{1,0:T(8,128)}, u32[]{:S(2)}) copy-start(f32[64,4096]{1,0:T(8,128)} %get-tuple-element.34) | copy-start | bytes 3145732
  60.2 14.9 %collective-permute-start.8 = (bf16[32,4096]{1,0:T(8,128)(2,1)}, bf16[32,4096]{1,0:T(8,128)(2,1)S(1)}, u32[]{:S(2)}, u32[]{:S(2)}) collective-permute-start(bf16[32,4096]{1,0:T(8,128)(2,1)} %get-tuple-element.33), channel_id=1, source_target_pairs={{0,4},{1,5},{2,6},{3,7},{4,8},{5,9},{6,10},{7,11},{8,12},{9,13},{1... | collective-permute-start | bytes 786440 | tf_op jit(solution)/shard_map/sums/ppermute | solution.py:32
  61.8 15.4 %collective-permute-start.7 = (bf16[32,4096]{1,0:T(8,128)(2,1)}, bf16[32,4096]{1,0:T(8,128)(2,1)S(1)}, u32[]{:S(2)}, u32[]{:S(2)}) collective-permute-start(bf16[32,4096]{1,0:T(8,128)(2,1)} %get-tuple-element.32), channel_id=1, source_target_pairs={{0,8},{1,9},{2,10},{3,11},{4,12},{5,13},{6,14},{7,15},{8,0},{9,1},... | collective-permute-start | bytes 786440 | tf_op jit(solution)/shard_map/sums/ppermute | solution.py:32
  64.3 23.0 %collective-permute-start.6 = (bf16[32,4096]{1,0:T(8,128)(2,1)}, bf16[32,4096]{1,0:T(8,128)(2,1)S(1)}, u32[]{:S(2)}, u32[]{:S(2)}) collective-permute-start(bf16[32,4096]{1,0:T(8,128)(2,1)} %get-tuple-element.31), channel_id=1, source_target_pairs={{0,12},{1,13},{2,14},{3,15},{4,0},{5,1},{6,2},{7,3},{8,4},{9,5},{1... | collective-permute-start | bytes 786440 | tf_op jit(solution)/shard_map/sums/ppermute | solution.py:32
  64.4 25.1 %collective-permute-start.10 = (bf16[64,4096]{1,0:T(8,128)(2,1)}, bf16[64,4096]{1,0:T(8,128)(2,1)S(1)}, u32[]{:S(2)}, u32[]{:S(2)}) collective-permute-start(bf16[64,4096]{1,0:T(8,128)(2,1)} %get-tuple-element.35), channel_id=1, source_target_pairs={{0,2},{1,3},{2,0},{3,1},{4,6},{5,7},{6,4},{7,5},{8,10},{9,11},{10,... | collective-permute-start | bytes 1572872 | tf_op jit(solution)/shard_map/sums/ppermute | solution.py:32
  88.5 7.9 %collective-permute-start.9 = (bf16[16,4096]{1,0:T(8,128)(2,1)S(1)}, bf16[16,4096]{1,0:T(8,128)(2,1)S(1)}, u32[]{:S(2)}, u32[]{:S(2)}) collective-permute-start(bf16[16,4096]{1,0:T(8,128)(2,1)S(1)} %slice.145), channel_id=1, source_target_pairs={{0,2},{1,3},{2,0},{3,1},{4,6},{5,7},{6,4},{7,5},{8,10},{9,11},{10,... | collective-permute-start | bytes 393224 | tf_op jit(solution)/shard_map/sums/ppermute | solution.py:32
  89.7 7.9 %collective-permute-start.13 = (bf16[16,4096]{1,0:T(8,128)(2,1)S(1)}, bf16[16,4096]{1,0:T(8,128)(2,1)S(1)}, u32[]{:S(2)}, u32[]{:S(2)}) collective-permute-start(bf16[16,4096]{1,0:T(8,128)(2,1)S(1)} %get-tuple-element.60), channel_id=1, source_target_pairs={{0,4},{1,5},{2,6},{3,7},{4,8},{5,9},{6,10},{7,11},{8,12},{9,13},{1... | collective-permute-start | bytes 393224 | tf_op jit(solution)/shard_map/sums/ppermute | solution.py:32
  90.6 8.9 %collective-permute-start.12 = (bf16[16,4096]{1,0:T(8,128)(2,1)S(1)}, bf16[16,4096]{1,0:T(8,128)(2,1)S(1)}, u32[]{:S(2)}, u32[]{:S(2)}) collective-permute-start(bf16[16,4096]{1,0:T(8,128)(2,1)S(1)} %get-tuple-element.61), channel_id=1, source_target_pairs={{0,8},{1,9},{2,10},{3,11},{4,12},{5,13},{6,14},{7,15},{8,0},{9,1},... | collective-permute-start | bytes 393224 | tf_op jit(solution)/shard_map/sums/ppermute | solution.py:32
  93.1 21.9 %copy-start.11 = (s32[384]{0:T(512)S(1)}, s32[384]{0:T(512)}, u32[]{:S(2)}) copy-start(s32[384]{0:T(512)} %param.14) | copy-start | bytes 4612
  93.1 11.0 %collective-permute-start.11 = (bf16[16,4096]{1,0:T(8,128)(2,1)S(1)}, bf16[16,4096]{1,0:T(8,128)(2,1)S(1)}, u32[]{:S(2)}, u32[]{:S(2)}) collective-permute-start(bf16[16,4096]{1,0:T(8,128)(2,1)S(1)} %get-tuple-element.59), channel_id=1, source_target_pairs={{0,12},{1,13},{2,14},{3,15},{4,0},{5,1},{6,2},{7,3},{8,4},{9,5},{1... | collective-permute-start | bytes 393224 | tf_op jit(solution)/shard_map/sums/ppermute | solution.py:32
  105.4 21.5 %all-to-all-start = ((bf16[16,2,8320]{2,1,0:T(2,128)(2,1)}), bf16[16,2,8320]{2,1,0:T(2,128)(2,1)S(1)}, u32[]{:S(2)}, u32[]{:S(2)}) async-start(bf16[16,2,8320]{2,1,0:T(2,128)(2,1)} %reshape.61), calls=%async_computation | async-start | bytes 1064960 | tf_op jit(solution)/shard_map/route/all_to_all | solution.py:607
  114.9 107.5 %all-gather.5.cloned.1.call-start = ((), (), s32[]{:S(2)}) async-start(), calls=%async_computation.2 | async-start | bytes 3342336 | tf_op jit(solution)/shard_map/project/all_gather | solution.py:621
  127.1 15.0 %collective-permute-start.15 = (bf16[32,4096]{1,0:T(8,128)(2,1)S(1)}, bf16[32,4096]{1,0:T(8,128)(2,1)S(1)}, u32[]{:S(2)}, u32[]{:S(2)}) collective-permute-start(bf16[32,4096]{1,0:T(8,128)(2,1)S(1)} %slice.84), channel_id=1, source_target_pairs={{0,16},{16,0},{32,48},{48,32},{64,80},{80,64},{96,112},{112,96},{1... | collective-permute-start | bytes 786440 | tf_op jit(solution)/shard_map/route/ppermute | solution.py:44
  127.9 14.3 %collective-permute-start.18 = (bf16[32,4224]{1,0:T(8,128)(2,1)S(1)}, bf16[32,4224]{1,0:T(8,128)(2,1)S(1)}, u32[]{:S(2)}, u32[]{:S(2)}) collective-permute-start(bf16[32,4224]{1,0:T(8,128)(2,1)S(1)} %slice.85), channel_id=1, source_target_pairs={{0,96},{16,112},{32,0},{48,16},{64,32},{80,48},{96,64},{112,80},{1... | collective-permute-start | bytes 811016 | tf_op jit(solution)/shard_map/route/ppermute | solution.py:44
  128.2 14.0 %collective-permute-start.17 = (bf16[32,4224]{1,0:T(8,128)(2,1)S(1)}, bf16[32,4224]{1,0:T(8,128)(2,1)S(1)}, u32[]{:S(2)}, u32[]{:S(2)}) collective-permute-start(bf16[32,4224]{1,0:T(8,128)(2,1)S(1)} %slice.85), channel_id=1, source_target_pairs={{0,64},{16,80},{32,96},{48,112},{64,0},{80,16},{96,32},{112,48},{1... | collective-permute-start | bytes 811016 | tf_op jit(solution)/shard_map/route/ppermute | solution.py:44
  131.8 12.8 %collective-permute-start.16 = (bf16[32,4224]{1,0:T(8,128)(2,1)S(1)}, bf16[32,4224]{1,0:T(8,128)(2,1)S(1)}, u32[]{:S(2)}, u32[]{:S(2)}) collective-permute-start(bf16[32,4224]{1,0:T(8,128)(2,1)S(1)} %slice.85), channel_id=1, source_target_pairs={{0,32},{16,48},{32,64},{48,80},{64,96},{80,112},{96,0},{112,16},{1... | collective-permute-start | bytes 811016 | tf_op jit(solution)/shard_map/route/ppermute | solution.py:44
  142.2 31.1 %copy-start.1 = (bf16[64,4096]{1,0:T(8,128)(2,1)}, bf16[64,4096]{1,0:T(8,128)(2,1)S(1)}, u32[]{:S(2)}) copy-start(bf16[64,4096]{1,0:T(8,128)(2,1)S(1)} %pad_maximum_fusion.2.a0) | copy-start | bytes 1572868
  144.7 28.7 %copy-start = (bf16[128,4224]{1,0:T(8,128)(2,1)}, bf16[128,4224]{1,0:T(8,128)(2,1)S(1)}, u32[]{:S(2)}) copy-start(bf16[128,4224]{1,0:T(8,128)(2,1)S(1)} %pad_maximum_fusion.1.b0) | copy-start | bytes 3244036
  144.7 35.0 %collective-permute-start.22 = (bf16[128,4224]{1,0:T(8,128)(2,1)S(1)}, bf16[128,4224]{1,0:T(8,128)(2,1)S(1)}, u32[]{:S(2)}, u32[]{:S(2)}) collective-permute-start(bf16[128,4224]{1,0:T(8,128)(2,1)S(1)} %pad_maximum_fusion.1.b0), channel_id=1, source_target_pairs={{0,16},{16,0},{32,48},{48,32},{64,80},{80,64},{96,112},{112,96},{1... | collective-permute-start | bytes 3244040 | tf_op jit(solution)/shard_map/route/ppermute | solution.py:44
  147.0 26.4 %collective-permute-start.19 = (bf16[64,4096]{1,0:T(8,128)(2,1)S(1)}, bf16[64,4096]{1,0:T(8,128)(2,1)S(1)}, u32[]{:S(2)}, u32[]{:S(2)}) collective-permute-start(bf16[64,4096]{1,0:T(8,128)(2,1)S(1)} %pad_maximum_fusion.2.a0), channel_id=1, source_target_pairs={{0,32},{16,48},{32,64},{48,80},{64,96},{80,112},{96,0},{112,16},{1... | collective-permute-start | bytes 1572872 | tf_op jit(solution)/shard_map/route/ppermute | solution.py:44
  147.0 26.4 %collective-permute-start.20 = (bf16[64,4096]{1,0:T(8,128)(2,1)S(1)}, bf16[64,4096]{1,0:T(8,128)(2,1)}, u32[]{:S(2)}, u32[]{:S(2)}) collective-permute-start(bf16[64,4096]{1,0:T(8,128)(2,1)S(1)} %pad_maximum_fusion.2.a0), channel_id=1, source_target_pairs={{0,64},{16,80},{32,96},{48,112},{64,0},{80,16},{96,32},{112,48},{1... | collective-permute-start | bytes 1572872 | tf_op jit(solution)/shard_map/route/ppermute | solution.py:44
  149.2 24.2 %collective-permute-start.21 = (bf16[64,4096]{1,0:T(8,128)(2,1)S(1)}, bf16[64,4096]{1,0:T(8,128)(2,1)}, u32[]{:S(2)}, u32[]{:S(2)}) collective-permute-start(bf16[64,4096]{1,0:T(8,128)(2,1)S(1)} %pad_maximum_fusion.2.a0), channel_id=1, source_target_pairs={{0,96},{16,112},{32,0},{48,16},{64,32},{80,48},{96,64},{112,80},{1... | collective-permute-start | bytes 1572872 | tf_op jit(solution)/shard_map/route/ppermute | solution.py:44
  (7 other events, 50.6 us)
Sparse Core Ops, SparseCore 0:
  18.0 145.8 all-gather.2
  186.9 35.4 all-gather.4

commit v2 on v1

--- a/solution.py
+++ b/solution.py
@@ -204,10 +204,10 @@
     shape = jax.ShapeDtypeStruct
     return pl.pallas_call(
         text_kernel,
-        grid=(width // CHUNK,),
+        grid=(width // SLOT_CHUNK,),
         in_specs=[
-            pl.BlockSpec((rows, CHUNK), lambda n: (0, n)),
-            pl.BlockSpec((CHUNK, 2 * HD), lambda n: (n, kv_block)),
+            pl.BlockSpec((rows, SLOT_CHUNK), lambda n: (0, n)),
+            pl.BlockSpec((SLOT_CHUNK, 2 * HD), lambda n: (n, kv_block)),
         ],
         out_specs=[whole((rows, 2 * HD)), whole((rows, HD))],
         out_shape=[shape((rows, 2 * HD), jnp.float32), shape((rows, HD), jnp.float32)],
@@ -305,7 +305,6 @@
 GROUP = 2
 SOFT = HD ** (-0.5) * LOG2E
 LIMIT = 60.0
-STEP = 4
 
 
 def query_kernel(
@@ -464,29 +463,21 @@
 
     start()
     base_ref[...] = top_in[...] * SOFT
-    plain = me - clear
-
-    def step(i, _):
-        at = me - 1 - STEP * i
-        fast([at - n for n in range(STEP)], False)
-        return 0
-
-    lax.fori_loop(0, plain // STEP, step, 0)
-    left = plain % STEP
-
-    @pl.when(left >= 2)
-    def _():
-        fast([clear + left - 1, clear + left - 2], False)
-
-    @pl.when(left % 2 == 1)
-    def _():
-        fast([clear], False)
-
-    def masked_step(i, _):
-        fast([clear - 1 - i], True)
-        return 0
-
-    lax.fori_loop(0, clear - first, masked_step, 0)
+    def run(low, high, wide_step, masked):
+        def several(i, _):
+            at = high - 1 - wide_step * i
+            fast([at - n for n in range(wide_step)], masked)
+            return 0
+
+        def single(i, _):
+            fast([low + i], masked)
+            return 0
+
+        lax.fori_loop(0, (high - low) // wide_step, several, 0)
+        lax.fori_loop(0, (high - low) % wide_step, single, 0)
+
+    run(clear, me, 4, False)
+    run(first, clear, 2, True)
     grown = jnp.max(top_ref[...] * SOFT - base_ref[...])
 
     @pl.when(grown > LIMIT)

time: 284 us -> 303 us (1.067)
  the two profiles are of different devices: /device:TPU:95 before, /device:TPU:23 now
where the time goes in v2:
time: 303 us
  Pallas kernels  117 us (39%)
  waiting for transfers between devices  115 us (38%)
  starting transfers between devices  40 us (13%)
  between operations  16.5 us (5%)
  other arithmetic  8.55 us (3%)
  local copies, waits for them, and re-layouts  5.13 us (2%)
    pallas_call x1, Pallas kernels, attend(): pl.pallas_call(attention_kernel, in_specs=[pl.BlockSpec(memory_space=pltp...  72 us
    ppermute x15, waiting for transfers between devices, seq_shift(): return lax.ppermute(array, SEQ, pairs)  57 us
    ppermute x8, waiting for transfers between devices, pool_shift(): return lax.ppermute(array, POOL, pairs)  21.6 us
    pallas_call x1, Pallas kernels, query(): pl.pallas_call(query_kernel, grid=(width // CHUNK,), in_specs=[pl.BlockSp...  19.7 us
    ppermute x15, starting transfers between devices, seq_shift(): return lax.ppermute(array, SEQ, pairs)  19.3 us
    all_gather x1, waiting for transfers between devices, per_device(): kv_all = lax.all_gather(kv, SEQ, axis=0, tiled=True)  18.4 us
    ppermute x8, starting transfers between devices, pool_shift(): return lax.ppermute(array, POOL, pairs)  11.8 us
    pallas_call x1, Pallas kernels, merger(): pl.pallas_call(merger_kernel, in_specs=[VMEM] * X + [ANY] * 4, out_specs=...  9.63 us
  transfers between devices with their start and end apart: 26, of which 20 were waited for; matrix products, arithmetic and copies ran while one was open for 3% of the time, Pallas kernels for 12%

profile of v2, /device:TPU:23, one launch (start us, length us, event | category | flops | bytes accessed | tf_op | source)
XLA Modules:
  0.0 302.8 jit_solution(6139677588626673131)
XLA Ops:
  7.9 1.9 prepare.1
  10.9 4.5 %collective-permute-done = bf16[16,5248]{1,0:T(8,128)(2,1)} collective-permute-done((bf16[16,5248]{1,0:T(8,128)(2,1)}, bf16[16,5248]{1,0:T(8,128)(2,1)}, u32[]{:S(2)}, u32[]{:S(2)}) %collective-permute-start) | collective-permute-done | bytes 167968 | tf_op jit(solution)/shard_map/merger/ppermute | solution.py:32
  15.3 2.5 pad_maximum_fusion
  21.3 2.1 collective-permute-start.2
  24.3 5.9 %collective-permute-done.1.refs_1_ = bf16[32,5248]{1,0:T(8,128)(2,1)S(1)} collective-permute-done((bf16[32,5248]{1,0:T(8,128)(2,1)S(1)}, bf16[32,5248]{1,0:T(8,128)(2,1)S(1)}, u32[]{:S(2)}, u32[]{:S(2)}) %collective-permute-start.1) | collective-permute-done | bytes 335904 | tf_op jit(solution)/shard_map/merger/ppermute | solution.py:32
  31.6 12.4 %collective-permute-done.3.refs_3_ = bf16[32,5248]{1,0:T(8,128)(2,1)S(1)} collective-permute-done((bf16[32,5248]{1,0:T(8,128)(2,1)S(1)}, bf16[32,5248]{1,0:T(8,128)(2,1)S(1)}, u32[]{:S(2)}, u32[]{:S(2)}) %collective-permute-start.3) | collective-permute-done | bytes 335904 | tf_op jit(solution)/shard_map/merger/ppermute | solution.py:32
  44.7 3.8 %collective-permute-start.14 = (f32[1,128]{1,0:T(1,128)S(1)}, f32[1,128]{1,0:T(1,128)S(1)}, u32[]{:S(2)}, u32[]{:S(2)}) collective-permute-start(f32[1,128]{1,0:T(1,128)S(1)} %fusion.16), channel_id=1, source_target_pairs={{0,1},{1,0},{2,3},{3,2},{4,5},{5,4},{6,7},{7,6},{8,9},{9,8},{10,11... | collective-permute-start | bytes 1544 | tf_op jit(solution)/shard_map/segments/ppermute | solution.py:32
  49.6 9.6 %merger.1 = (f32[32,4096]{1,0:T(8,128)}, bf16[32,4096]{1,0:T(8,128)(2,1)}, bf16[32,4096]{1,0:T(8,128)(2,1)}, bf16[32,4096]{1,0:T(8,128)(2,1)}, f32[64,4096]{1,0:T(8,128)}, /*index=5*/bf16[64,4096]{1,0:T(8,128)(2,1)}) custom-call(bf16[32,5248]{1,0:T(8,128)(2,1)} %copy-done.5, bf16[32,5248]{1,0:T(8,128)(2,1)} %copy-done.8, bf16[32,5248]{1,0:T(8,128)(2,1)} %copy-done.9, ...), custom_call_target="tpu_custom_call" | custom-call | tf_op jit(solution)/shard_map/merger/merger/pallas_call | solution.py:137
  61.0 2.4 collective-permute-start.7
  64.6 9.7 %collective-permute-done.8 = bf16[32,4096]{1,0:T(8,128)(2,1)S(1)} collective-permute-done((bf16[32,4096]{1,0:T(8,128)(2,1)}, bf16[32,4096]{1,0:T(8,128)(2,1)S(1)}, u32[]{:S(2)}, u32[]{:S(2)}) %collective-permute-start.8) | collective-permute-done | bytes 262176 | tf_op jit(solution)/shard_map/sums/ppermute | solution.py:32
  74.2 2.1 collective-permute-done.7
  76.4 10.0 %collective-permute-done.6 = bf16[32,4096]{1,0:T(8,128)(2,1)S(1)} collective-permute-done((bf16[32,4096]{1,0:T(8,128)(2,1)}, bf16[32,4096]{1,0:T(8,128)(2,1)S(1)}, u32[]{:S(2)}, u32[]{:S(2)}) %collective-permute-start.6) | collective-permute-done | bytes 262176 | tf_op jit(solution)/shard_map/sums/ppermute | solution.py:32
  88.8 1.8 collective-permute-start.13
  90.6 2.3 collective-permute-start.12
  92.8 2.6 collective-permute-done.9
  95.5 2.0 collective-permute-done.13
  97.4 2.2 collective-permute-done.12
  99.6 4.2 %collective-permute-done.11 = bf16[16,4096]{1,0:T(8,128)(2,1)S(1)} collective-permute-done((bf16[16,4096]{1,0:T(8,128)(2,1)S(1)}, bf16[16,4096]{1,0:T(8,128)(2,1)S(1)}, u32[]{:S(2)}, u32[]{:S(2)}) %collective-permute-start.11) | collective-permute-done | bytes 131104 | tf_op jit(solution)/shard_map/sums/ppermute | solution.py:32
  105.1 8.9 %all-to-all-start = ((bf16[16,2,8320]{2,1,0:T(2,128)(2,1)}), bf16[16,2,8320]{2,1,0:T(2,128)(2,1)S(1)}, u32[]{:S(2)}, u32[]{:S(2)}) async-start(bf16[16,2,8320]{2,1,0:T(2,128)(2,1)} %reshape.61), calls=%async_computation | async-start | bytes 1064960 | tf_op jit(solution)/shard_map/route/all_to_all | solution.py:598
  118.7 9.4 %all-to-all-done = bf16[16,2,8320]{2,1,0:T(2,128)(2,1)S(1)} async-done(((bf16[16,2,8320]{2,1,0:T(2,128)(2,1)}), bf16[16,2,8320]{2,1,0:T(2,128)(2,1)S(1)}, u32[]{:S(2)}, u32[]{:S(2)}) %all-to-all-start) | async-done | bytes 532512 | tf_op jit(solution)/shard_map/route/all_to_all | solution.py:598
  128.5 5.3 %collective-permute-start.18 = (bf16[32,4224]{1,0:T(8,128)(2,1)S(1)}, bf16[32,4224]{1,0:T(8,128)(2,1)S(1)}, u32[]{:S(2)}, u32[]{:S(2)}) collective-permute-start(bf16[32,4224]{1,0:T(8,128)(2,1)S(1)} %slice.85), channel_id=1, source_target_pairs={{0,96},{16,112},{32,0},{48,16},{64,32},{80,48},{96,64},{112,80},{1... | collective-permute-start | bytes 811016 | tf_op jit(solution)/shard_map/route/ppermute | solution.py:44
  134.4 9.0 %collective-permute-done.15 = bf16[32,4096]{1,0:T(8,128)(2,1)S(1)} collective-permute-done((bf16[32,4096]{1,0:T(8,128)(2,1)S(1)}, bf16[32,4096]{1,0:T(8,128)(2,1)S(1)}, u32[]{:S(2)}, u32[]{:S(2)}) %collective-permute-start.15) | collective-permute-done | bytes 262176 | tf_op jit(solution)/shard_map/route/ppermute | solution.py:44
  144.4 4.4 %collective-permute-done.16 = bf16[32,4224]{1,0:T(8,128)(2,1)S(1)} collective-permute-done((bf16[32,4224]{1,0:T(8,128)(2,1)S(1)}, bf16[32,4224]{1,0:T(8,128)(2,1)S(1)}, u32[]{:S(2)}, u32[]{:S(2)}) %collective-permute-start.16) | collective-permute-done | bytes 270368 | tf_op jit(solution)/shard_map/route/ppermute | solution.py:44
  148.9 2.9 collective-permute-start.22
  152.6 2.1 collective-permute-start.21
  154.7 8.7 %all-gather.3.cloned.1.call-done.weight_ref = bf16[8192,1280]{1,0:T(8,128)(2,1)} async-done(((bf16[512,1280]{1,0:T(8,128)(2,1)}), bf16[8192,1280]{1,0:T(8,128)(2,1)}) %all-gather.3.cloned.1.call-update) | async-done | bytes 20971536 | tf_op jit(solution)/shard_map/merger/all_gather | solution.py:544
  163.3 8.0 %project_text.1 = (f32[384,256]{1,0:T(8,128)}, f32[384,128]{1,0:T(8,128)}) custom-call(bf16[384,8192]{1,0:T(8,128)(2,1)} %text_ref.2, bf16[8192,1280]{1,0:T(8,128)(2,1)} %all-gather.3.cloned.1.call-done.weight_ref), custom_call_target="tpu_custom_call" | custom-call | tf_op jit(solution)/shard_map/project/project_text/pallas_call | solution.py:205
  171.4 5.2 %collective-permute-done.19.a1 = bf16[64,4096]{1,0:T(8,128)(2,1)S(1)} collective-permute-done((bf16[64,4096]{1,0:T(8,128)(2,1)S(1)}, bf16[64,4096]{1,0:T(8,128)(2,1)S(1)}, u32[]{:S(2)}, u32[]{:S(2)}) %collective-permute-start.19) | collective-permute-done | bytes 524320 | tf_op jit(solution)/shard_map/route/ppermute | solution.py:44
  179.6 6.1 %project_slots.1 = (bf16[384,256]{1,0:T(8,128)(2,1)}, f32[384,128]{1,0:T(8,128)}) custom-call(bf16[64,4096]{1,0:T(8,128)(2,1)} %copy-done.1, bf16[64,4096]{1,0:T(8,128)(2,1)} %copy-done.4, bf16[64,4096]{1,0:T(8,128)(2,1)} %collective-permute-done.20.a2, bf16[64,4096]{1,0:T(8,128)(2,1)} %collective-permute-done.21.a3, bf16[128,4224]{1,0:T(8,128)(2,1)} %copy-done, ...), custom_call_target="tpu_custom_call" | custom-call | tf_op jit(solution)/shard_map/project/project_slots/pallas_call | solution.py:287
  185.8 19.7 %query.1 = (bf16[3072,128]{1,0:T(8,128)(2,1)}, f32[1,3072]{1,0:T(1,128)}, f32[1,3072]{1,0:T(1,128)}, f32[128,3072]{1,0:T(8,128)}) custom-call(bf16[384,8192]{1,0:T(8,128)(2,1)} %text_ref.2, bf16[64,4096]{1,0:T(8,128)(2,1)} %copy-done.1, bf16[64,4096]{1,0:T(8,128)(2,1)} %copy-done.4, bf16[64,4096]{1,0:T(8,128)(2,1)} %collective-permute-done.20.a2, ...), custom_call_target="tpu_custom_call" | custom-call | tf_op jit(solution)/shard_map/project/query/pallas_call | solution.py:373
  205.5 18.4 %all-gather.5.cloned.1.call-done = bf16[6144,256]{1,0:T(8,128)(2,1)} async-done(((bf16[384,256]{1,0:T(8,128)(2,1)}), bf16[6144,256]{1,0:T(8,128)(2,1)}) %all-gather.5.cloned.1.call-update) | async-done | bytes 3145744 | tf_op jit(solution)/shard_map/project/all_gather | solution.py:612
  223.8 72.0 %attend.1 = bf16[384,1024]{1,0:T(8,128)(2,1)} custom-call(s32[3]{0:T(128)} %pad_add_fusion.1.info_ref, bf16[3072,128]{1,0:T(8,128)(2,1)} %get-tuple-element.51.q_ref, f32[1,3072]{1,0:T(1,128)} %get-tuple-element.52.top_in, f32[1,3072]{1,0:T(1,128)} %get-tuple-element.53.sum_in, f32[128,3072]{1,0:T(8,128)} %get-tuple-element.54.acc_in, ...), custom_call_target="tpu_custom_call" | custom-call | tf_op jit(solution)/shard_map/attend/attend/pallas_call | solution.py:502
  (92 shorter events, 24.4 us)
Async XLA Ops:
  6.5 156.8 %all-gather.3.cloned.1.call-start = ((), (), s32[]{:S(2)}) async-start(), calls=%async_computation.1 | async-start | bytes 22282240 | tf_op jit(solution)/shard_map/merger/all_gather | solution.py:544
  9.9 5.5 %collective-permute-start = (bf16[16,5248]{1,0:T(8,128)(2,1)}, bf16[16,5248]{1,0:T(8,128)(2,1)}, u32[]{:S(2)}, u32[]{:S(2)}) collective-permute-start(bf16[16,5248]{1,0:T(8,128)(2,1)} %prepare.1), channel_id=1, source_target_pairs={{0,2},{1,3},{2,0},{3,1},{4,6},{5,7},{6,4},{7,5},{8,10},{9,11},{10,... | collective-permute-start | bytes 503816 | tf_op jit(solution)/shard_map/merger/ppermute | solution.py:32
  17.9 31.7 %collective-permute-start.5 = (bf16[320,8192]{1,0:T(8,128)(2,1)}, bf16[320,8192]{1,0:T(8,128)(2,1)}, u32[]{:S(2)}, u32[]{:S(2)}) collective-permute-start(bf16[320,8192]{1,0:T(8,128)(2,1)} %refs_6_.1), channel_id=1, source_target_pairs={{0,1},{1,0},{2,3},{3,2},{4,5},{5,4},{6,7},{7,6},{8,9},{9,8},{10,11... | collective-permute-start | bytes 15728648 | tf_op jit(solution)/shard_map/merger/ppermute | solution.py:32
  19.5 30.1 %collective-permute-start.4 = (bf16[320,5120]{1,0:T(8,128)(2,1)S(1)}, bf16[320,5120]{1,0:T(8,128)(2,1)}, u32[]{:S(2)}, u32[]{:S(2)}) collective-permute-start(bf16[320,5120]{1,0:T(8,128)(2,1)S(1)} %bitcast.17), channel_id=1, source_target_pairs={{0,1},{1,0},{2,3},{3,2},{4,5},{5,4},{6,7},{7,6},{8,9},{9,8},{10,11... | collective-permute-start | bytes 9830408 | tf_op jit(solution)/shard_map/merger/ppermute | solution.py:32
  21.1 9.1 %collective-permute-start.1 = (bf16[32,5248]{1,0:T(8,128)(2,1)S(1)}, bf16[32,5248]{1,0:T(8,128)(2,1)S(1)}, u32[]{:S(2)}, u32[]{:S(2)}) collective-permute-start(bf16[32,5248]{1,0:T(8,128)(2,1)S(1)} %pad_maximum_fusion.3.refs_0_), channel_id=1, source_target_pairs={{0,4},{1,5},{2,6},{3,7},{4,8},{5,9},{6,10},{7,11},{8,12},{9,13},{1... | collective-permute-start | bytes 1007624 | tf_op jit(solution)/shard_map/merger/ppermute | solution.py:32
  21.3 10.3 %collective-permute-start.2 = (bf16[32,5248]{1,0:T(8,128)(2,1)S(1)}, bf16[32,5248]{1,0:T(8,128)(2,1)S(1)}, u32[]{:S(2)}, u32[]{:S(2)}) collective-permute-start(bf16[32,5248]{1,0:T(8,128)(2,1)S(1)} %pad_maximum_fusion.3.refs_0_), channel_id=1, source_target_pairs={{0,8},{1,9},{2,10},{3,11},{4,12},{5,13},{6,14},{7,15},{8,0},{9,1},... | collective-permute-start | bytes 1007624 | tf_op jit(solution)/shard_map/merger/ppermute | solution.py:32
  23.5 20.6 %collective-permute-start.3 = (bf16[32,5248]{1,0:T(8,128)(2,1)S(1)}, bf16[32,5248]{1,0:T(8,128)(2,1)S(1)}, u32[]{:S(2)}, u32[]{:S(2)}) collective-permute-start(bf16[32,5248]{1,0:T(8,128)(2,1)S(1)} %pad_maximum_fusion.3.refs_0_), channel_id=1, source_target_pairs={{0,12},{1,13},{2,14},{3,15},{4,0},{5,1},{6,2},{7,3},{8,4},{9,5},{1... | collective-permute-start | bytes 1007624 | tf_op jit(solution)/shard_map/merger/ppermute | solution.py:32
  30.2 14.5 %copy-start.8 = (bf16[32,5248]{1,0:T(8,128)(2,1)}, bf16[32,5248]{1,0:T(8,128)(2,1)S(1)}, u32[]{:S(2)}) copy-start(bf16[32,5248]{1,0:T(8,128)(2,1)S(1)} %collective-permute-done.1.refs_1_) | copy-start | bytes 1007620
  31.6 16.9 %copy-start.9 = (bf16[32,5248]{1,0:T(8,128)(2,1)}, bf16[32,5248]{1,0:T(8,128)(2,1)S(1)}, u32[]{:S(2)}) copy-start(bf16[32,5248]{1,0:T(8,128)(2,1)S(1)} %collective-permute-done.2.refs_2_) | copy-start | bytes 1007620
  44.7 4.8 %collective-permute-start.14 = (f32[1,128]{1,0:T(1,128)S(1)}, f32[1,128]{1,0:T(1,128)S(1)}, u32[]{:S(2)}, u32[]{:S(2)}) collective-permute-start(f32[1,128]{1,0:T(1,128)S(1)} %fusion.16), channel_id=1, source_target_pairs={{0,1},{1,0},{2,3},{3,2},{4,5},{5,4},{6,7},{7,6},{8,9},{9,8},{10,11... | collective-permute-start | bytes 1544 | tf_op jit(solution)/shard_map/segments/ppermute | solution.py:32
  59.2 29.4 %copy-start.6 = (f32[64,4096]{1,0:T(8,128)S(1)}, f32[64,4096]{1,0:T(8,128)}, u32[]{:S(2)}) copy-start(f32[64,4096]{1,0:T(8,128)} %get-tuple-element.34) | copy-start | bytes 3145732
  59.2 15.0 %collective-permute-start.8 = (bf16[32,4096]{1,0:T(8,128)(2,1)}, bf16[32,4096]{1,0:T(8,128)(2,1)S(1)}, u32[]{:S(2)}, u32[]{:S(2)}) collective-permute-start(bf16[32,4096]{1,0:T(8,128)(2,1)} %get-tuple-element.33), channel_id=1, source_target_pairs={{0,4},{1,5},{2,6},{3,7},{4,8},{5,9},{6,10},{7,11},{8,12},{9,13},{1... | collective-permute-start | bytes 786440 | tf_op jit(solution)/shard_map/sums/ppermute | solution.py:32
  61.0 15.4 %collective-permute-start.7 = (bf16[32,4096]{1,0:T(8,128)(2,1)}, bf16[32,4096]{1,0:T(8,128)(2,1)S(1)}, u32[]{:S(2)}, u32[]{:S(2)}) collective-permute-start(bf16[32,4096]{1,0:T(8,128)(2,1)} %get-tuple-element.32), channel_id=1, source_target_pairs={{0,8},{1,9},{2,10},{3,11},{4,12},{5,13},{6,14},{7,15},{8,0},{9,1},... | collective-permute-start | bytes 786440 | tf_op jit(solution)/shard_map/sums/ppermute | solution.py:32
  63.4 23.0 %collective-permute-start.6 = (bf16[32,4096]{1,0:T(8,128)(2,1)}, bf16[32,4096]{1,0:T(8,128)(2,1)S(1)}, u32[]{:S(2)}, u32[]{:S(2)}) collective-permute-start(bf16[32,4096]{1,0:T(8,128)(2,1)} %get-tuple-element.31), channel_id=1, source_target_pairs={{0,12},{1,13},{2,14},{3,15},{4,0},{5,1},{6,2},{7,3},{8,4},{9,5},{1... | collective-permute-start | bytes 786440 | tf_op jit(solution)/shard_map/sums/ppermute | solution.py:32
  63.5 25.1 %collective-permute-start.10 = (bf16[64,4096]{1,0:T(8,128)(2,1)}, bf16[64,4096]{1,0:T(8,128)(2,1)S(1)}, u32[]{:S(2)}, u32[]{:S(2)}) collective-permute-start(bf16[64,4096]{1,0:T(8,128)(2,1)} %get-tuple-element.35), channel_id=1, source_target_pairs={{0,2},{1,3},{2,0},{3,1},{4,6},{5,7},{6,4},{7,5},{8,10},{9,11},{10,... | collective-permute-start | bytes 1572872 | tf_op jit(solution)/shard_map/sums/ppermute | solution.py:32
  87.5 7.9 %collective-permute-start.9 = (bf16[16,4096]{1,0:T(8,128)(2,1)S(1)}, bf16[16,4096]{1,0:T(8,128)(2,1)S(1)}, u32[]{:S(2)}, u32[]{:S(2)}) collective-permute-start(bf16[16,4096]{1,0:T(8,128)(2,1)S(1)} %slice.145), channel_id=1, source_target_pairs={{0,2},{1,3},{2,0},{3,1},{4,6},{5,7},{6,4},{7,5},{8,10},{9,11},{10,... | collective-permute-start | bytes 393224 | tf_op jit(solution)/shard_map/sums/ppermute | solution.py:32
  88.8 8.6 %collective-permute-start.13 = (bf16[16,4096]{1,0:T(8,128)(2,1)S(1)}, bf16[16,4096]{1,0:T(8,128)(2,1)S(1)}, u32[]{:S(2)}, u32[]{:S(2)}) collective-permute-start(bf16[16,4096]{1,0:T(8,128)(2,1)S(1)} %get-tuple-element.60), channel_id=1, source_target_pairs={{0,4},{1,5},{2,6},{3,7},{4,8},{5,9},{6,10},{7,11},{8,12},{9,13},{1... | collective-permute-start | bytes 393224 | tf_op jit(solution)/shard_map/sums/ppermute | solution.py:32
  90.6 9.0 %collective-permute-start.12 = (bf16[16,4096]{1,0:T(8,128)(2,1)S(1)}, bf16[16,4096]{1,0:T(8,128)(2,1)S(1)}, u32[]{:S(2)}, u32[]{:S(2)}) collective-permute-start(bf16[16,4096]{1,0:T(8,128)(2,1)S(1)} %get-tuple-element.61), channel_id=1, source_target_pairs={{0,8},{1,9},{2,10},{3,11},{4,12},{5,13},{6,14},{7,15},{8,0},{9,1},... | collective-permute-start | bytes 393224 | tf_op jit(solution)/shard_map/sums/ppermute | solution.py:32
  92.8 21.2 %copy-start.11 = (s32[384]{0:T(512)S(1)}, s32[384]{0:T(512)}, u32[]{:S(2)}) copy-start(s32[384]{0:T(512)} %param.14) | copy-start | bytes 4612
  92.8 11.0 %collective-permute-start.11 = (bf16[16,4096]{1,0:T(8,128)(2,1)S(1)}, bf16[16,4096]{1,0:T(8,128)(2,1)S(1)}, u32[]{:S(2)}, u32[]{:S(2)}) collective-permute-start(bf16[16,4096]{1,0:T(8,128)(2,1)S(1)} %get-tuple-element.59), channel_id=1, source_target_pairs={{0,12},{1,13},{2,14},{3,15},{4,0},{5,1},{6,2},{7,3},{8,4},{9,5},{1... | collective-permute-start | bytes 393224 | tf_op jit(solution)/shard_map/sums/ppermute | solution.py:32
  105.1 23.0 %all-to-all-start = ((bf16[16,2,8320]{2,1,0:T(2,128)(2,1)}), bf16[16,2,8320]{2,1,0:T(2,128)(2,1)S(1)}, u32[]{:S(2)}, u32[]{:S(2)}) async-start(bf16[16,2,8320]{2,1,0:T(2,128)(2,1)} %reshape.61), calls=%async_computation | async-start | bytes 1064960 | tf_op jit(solution)/shard_map/route/all_to_all | solution.py:598
  114.0 109.8 %all-gather.5.cloned.1.call-start = ((), (), s32[]{:S(2)}) async-start(), calls=%async_computation.2 | async-start | bytes 3342336 | tf_op jit(solution)/shard_map/project/all_gather | solution.py:612
  128.4 15.1 %collective-permute-start.15 = (bf16[32,4096]{1,0:T(8,128)(2,1)S(1)}, bf16[32,4096]{1,0:T(8,128)(2,1)S(1)}, u32[]{:S(2)}, u32[]{:S(2)}) collective-permute-start(bf16[32,4096]{1,0:T(8,128)(2,1)S(1)} %slice.84), channel_id=1, source_target_pairs={{0,16},{16,0},{32,48},{48,32},{64,80},{80,64},{96,112},{112,96},{1... | collective-permute-start | bytes 786440 | tf_op jit(solution)/shard_map/route/ppermute | solution.py:44
  128.5 15.9 %collective-permute-start.18 = (bf16[32,4224]{1,0:T(8,128)(2,1)S(1)}, bf16[32,4224]{1,0:T(8,128)(2,1)S(1)}, u32[]{:S(2)}, u32[]{:S(2)}) collective-permute-start(bf16[32,4224]{1,0:T(8,128)(2,1)S(1)} %slice.85), channel_id=1, source_target_pairs={{0,96},{16,112},{32,0},{48,16},{64,32},{80,48},{96,64},{112,80},{1... | collective-permute-start | bytes 811016 | tf_op jit(solution)/shard_map/route/ppermute | solution.py:44
  133.8 10.7 %collective-permute-start.17 = (bf16[32,4224]{1,0:T(8,128)(2,1)S(1)}, bf16[32,4224]{1,0:T(8,128)(2,1)S(1)}, u32[]{:S(2)}, u32[]{:S(2)}) collective-permute-start(bf16[32,4224]{1,0:T(8,128)(2,1)S(1)} %slice.85), channel_id=1, source_target_pairs={{0,64},{16,80},{32,96},{48,112},{64,0},{80,16},{96,32},{112,48},{1... | collective-permute-start | bytes 811016 | tf_op jit(solution)/shard_map/route/ppermute | solution.py:44
  133.8 15.1 %collective-permute-start.16 = (bf16[32,4224]{1,0:T(8,128)(2,1)S(1)}, bf16[32,4224]{1,0:T(8,128)(2,1)S(1)}, u32[]{:S(2)}, u32[]{:S(2)}) collective-permute-start(bf16[32,4224]{1,0:T(8,128)(2,1)S(1)} %slice.85), channel_id=1, source_target_pairs={{0,32},{16,48},{32,64},{48,80},{64,96},{80,112},{96,0},{112,16},{1... | collective-permute-start | bytes 811016 | tf_op jit(solution)/shard_map/route/ppermute | solution.py:44
  143.5 27.9 %copy-start.1 = (bf16[64,4096]{1,0:T(8,128)(2,1)}, bf16[64,4096]{1,0:T(8,128)(2,1)S(1)}, u32[]{:S(2)}) copy-start(bf16[64,4096]{1,0:T(8,128)(2,1)S(1)} %pad_maximum_fusion.2.a0) | copy-start | bytes 1572868
  148.9 22.5 %copy-start = (bf16[128,4224]{1,0:T(8,128)(2,1)}, bf16[128,4224]{1,0:T(8,128)(2,1)S(1)}, u32[]{:S(2)}) copy-start(bf16[128,4224]{1,0:T(8,128)(2,1)S(1)} %pad_maximum_fusion.1.b0) | copy-start | bytes 3244036
  148.9 29.7 %collective-permute-start.22 = (bf16[128,4224]{1,0:T(8,128)(2,1)S(1)}, bf16[128,4224]{1,0:T(8,128)(2,1)S(1)}, u32[]{:S(2)}, u32[]{:S(2)}) collective-permute-start(bf16[128,4224]{1,0:T(8,128)(2,1)S(1)} %pad_maximum_fusion.1.b0), channel_id=1, source_target_pairs={{0,16},{16,0},{32,48},{48,32},{64,80},{80,64},{96,112},{112,96},{1... | collective-permute-start | bytes 3244040 | tf_op jit(solution)/shard_map/route/ppermute | solution.py:44
  151.8 24.7 %collective-permute-start.19 = (bf16[64,4096]{1,0:T(8,128)(2,1)S(1)}, bf16[64,4096]{1,0:T(8,128)(2,1)S(1)}, u32[]{:S(2)}, u32[]{:S(2)}) collective-permute-start(bf16[64,4096]{1,0:T(8,128)(2,1)S(1)} %pad_maximum_fusion.2.a0), channel_id=1, source_target_pairs={{0,32},{16,48},{32,64},{48,80},{64,96},{80,112},{96,0},{112,16},{1... | collective-permute-start | bytes 1572872 | tf_op jit(solution)/shard_map/route/ppermute | solution.py:44
  151.8 24.7 %collective-permute-start.20 = (bf16[64,4096]{1,0:T(8,128)(2,1)S(1)}, bf16[64,4096]{1,0:T(8,128)(2,1)}, u32[]{:S(2)}, u32[]{:S(2)}) collective-permute-start(bf16[64,4096]{1,0:T(8,128)(2,1)S(1)} %pad_maximum_fusion.2.a0), channel_id=1, source_target_pairs={{0,64},{16,80},{32,96},{48,112},{64,0},{80,16},{96,32},{112,48},{1... | collective-permute-start | bytes 1572872 | tf_op jit(solution)/shard_map/route/ppermute | solution.py:44
  152.6 24.8 %collective-permute-start.21 = (bf16[64,4096]{1,0:T(8,128)(2,1)S(1)}, bf16[64,4096]{1,0:T(8,128)(2,1)}, u32[]{:S(2)}, u32[]{:S(2)}) collective-permute-start(bf16[64,4096]{1,0:T(8,128)(2,1)S(1)} %pad_maximum_fusion.2.a0), channel_id=1, source_target_pairs={{0,96},{16,112},{32,0},{48,16},{64,32},{80,48},{96,64},{112,80},{1... | collective-permute-start | bytes 1572872 | tf_op jit(solution)/shard_map/route/ppermute | solution.py:44
  (7 other events, 46.4 us)
Sparse Core Ops, SparseCore 0:
  18.0 145.2 all-gather.2
  185.9 37.8 all-gather.4
